TPU v7x, 32 devices: a whole 2x2x4 slice. The times are simulated.
32 devices in a mesh: frame: 4 (over y, x), clip: 8 (over z, core).
Axes of the slice: x: 2, y: 2, z: 4, core: 2. Of those that a mesh axis runs over, the one named last changes fastest.
Arguments:
- tokens: bfloat16 [32, 1568, 384], P('clip', 'frame'), may hold values from -6 to 6
- out_grad: bfloat16 [32, 1568, 384], P('clip', 'frame'), may hold values from -6 to 6
- view_masks: int32 [32, 2, 1568], P('clip', None, 'frame'), may hold values from 0 to 1
- view_group: int32 [32, 2], P('clip'), may hold values from 0 to 1
- w_qkv: bfloat16 [384, 1152], replicated, may hold values from -0.3125 to 0.3125
- query_bias: float32 [384], replicated, may hold values from -3 to 3
- value_bias: float32 [384], replicated, may hold values from -3 to 3
- w_proj: bfloat16 [384, 384], replicated, may hold values from -2.5 to 2.5
- proj_bias: float32 [384], replicated, may hold values from -2 to 2
- w_up: bfloat16 [384, 1536], replicated, may hold values from -0.3125 to 0.3125
- up_bias: float32 [1536], replicated, may hold values from -3 to 3
- w_down: bfloat16 [1536, 384], replicated, may hold values from -0.15625 to 0.15625
- down_bias: float32 [384], replicated, may hold values from -2 to 2
- gain_one: float32 [384], replicated, may hold values from 0.25 to 1.75
- shift_one: float32 [384], replicated, may hold values from -2 to 2
- gain_two: float32 [384], replicated, may hold values from 0.25 to 1.75
- shift_two: float32 [384], replicated, may hold values from -2 to 2
Outputs:
- block_out: bfloat16 [32, 1568, 384], P('clip', 'frame')
- group_stats: float32 [32, 2, 2, 384], P('clip')
- grad_tokens: bfloat16 [32, 1568, 384], P('clip', 'frame')
- grad_w_qkv: float32 [384, 1152], replicated
- grad_query_bias: float32 [384], replicated
- grad_value_bias: float32 [384], replicated
- grad_w_proj: float32 [384, 384], replicated
- grad_proj_bias: float32 [384], replicated
- grad_w_up: float32 [384, 1536], replicated
- grad_up_bias: float32 [1536], replicated
- grad_w_down: float32 [1536, 384], replicated
- grad_down_bias: float32 [384], replicated
- grad_gain_one: float32 [384], replicated
- grad_shift_one: float32 [384], replicated
- grad_gain_two: float32 [384], replicated
- grad_shift_two: float32 [384], replicated
All inputs are finite; a program needn't handle non-finite values.
Results may differ from a plain program's by a relative error of at most 0.012.
Values may be sent and summed in bfloat16 or wider, within the bound.
A program may use at most 256 MiB of HBM per device.

v0:
```python
import jax
import jax.numpy as jnp
from jax import lax
from jax.sharding import PartitionSpec as P

HEADS = 6
NF = 8
HW = 196
GROUPS = 2


EPSILON = 1e-06
NEGATIVE = -1e30
HIGHEST = lax.Precision.HIGHEST


def with_halo(array, sides, width):
    for axis, dim in sides:
        count, length = (lax.axis_size(axis), array.shape[dim])
        up = [(i, (i + 1) % count) for i in range(count - 1)]
        down = [(j, i) for i, j in up]
        last = lax.slice_in_dim(array, length - width, length, axis=dim)
        leading = lax.slice_in_dim(array, 0, width, axis=dim)
        before = lax.ppermute(last, axis, up)
        after = lax.ppermute(leading, axis, down)
        array = jnp.concatenate([before, array, after], axis=dim)
    return array


def from_behind(block, axis, distance):
    devices = range(lax.axis_size(axis))
    route = [(i - distance, i) for i in devices if i - distance in devices]
    return lax.ppermute(block, axis, route)


def layer_norm(values_in, gain_vec, shift_vec):
    center = jnp.mean(values_in, axis=-1, keepdims=True)
    centered = values_in - center
    spread = jnp.mean(centered * centered, axis=-1, keepdims=True)
    return centered * lax.rsqrt(spread + EPSILON) * gain_vec + shift_vec


def gelu_exact(values_in):
    return jax.nn.gelu(values_in, approximate=False)


def group_weights(view_masks, view_group):
    member = (view_group[:, :, None] == jnp.arange(GROUPS, dtype=jnp.int32)[None, None, :]).astype(
        jnp.float32
    )
    return jnp.einsum("cvg,cvp->cpg", member, view_masks.astype(jnp.float32), precision=HIGHEST)


def group_sums(output_rows, weight_rows):
    counts = jnp.sum(weight_rows, axis=1)
    first_sums = jnp.einsum("cpg,cpd->cgd", weight_rows, output_rows, precision=HIGHEST)
    second_sums = jnp.einsum(
        "cpg,cpd->cgd", weight_rows, output_rows * output_rows, precision=HIGHEST
    )
    return (first_sums, second_sums, counts)


def group_moments(first_sums, second_sums, counts):
    floor_counts = jnp.maximum(counts, 1.0)[:, :, None]
    group_mean = first_sums / floor_counts
    group_var = second_sums / floor_counts - group_mean * group_mean
    return jnp.stack([group_mean, group_var], axis=2)


def layer(residual_in, out_grad, params, halo_rows, allowed, extend, fold):
    (
        w_qkv,
        query_bias,
        value_bias,
        w_proj,
        proj_bias,
        w_up,
        up_bias,
        w_down,
        down_bias,
        gain_one,
        shift_one,
        gain_two,
        shift_two,
    ) = params
    clip_count, row_count, model_width = residual_in.shape
    head_size = model_width // HEADS
    padded_rows = row_count + 2 * halo_rows
    score_scale = head_size ** (-0.5)
    normed_one, norm_back_one = jax.vjp(layer_norm, residual_in, gain_one, shift_one)
    normed_low = normed_one.astype(jnp.bfloat16)
    projected = jnp.einsum("cpd,de->cpe", normed_low, w_qkv, preferred_element_type=jnp.float32)
    queries = (projected[..., :model_width] + query_bias).astype(jnp.bfloat16)
    key_value = jnp.concatenate(
        [
            projected[..., model_width : 2 * model_width],
            projected[..., 2 * model_width :] + value_bias,
        ],
        axis=-1,
    ).astype(jnp.bfloat16)
    padded = extend(key_value)
    key_rows = padded[..., :model_width].reshape(clip_count, padded_rows, HEADS, head_size)
    value_rows = padded[..., model_width:].reshape(clip_count, padded_rows, HEADS, head_size)
    query_heads = queries.reshape(clip_count, row_count, HEADS, head_size)

    def scores_of(query_part, key_part):
        raw = (
            jnp.einsum("cqhd,ckhd->chqk", query_part, key_part, preferred_element_type=jnp.float32)
            * score_scale
        )
        return jnp.where(allowed[None, None], raw, NEGATIVE)

    scores = scores_of(query_heads, key_rows)
    top_score = jnp.max(scores, axis=-1, keepdims=True)
    log_total = top_score + jnp.log(jnp.sum(jnp.exp(scores - top_score), axis=-1, keepdims=True))
    probs_low = jnp.exp(scores - log_total).astype(jnp.bfloat16)
    context = jnp.einsum(
        "chqk,ckhd->cqhd", probs_low, value_rows, preferred_element_type=jnp.float32
    )
    context_low = context.reshape(clip_count, row_count, model_width).astype(jnp.bfloat16)
    attended = (
        jnp.einsum("cpd,de->cpe", context_low, w_proj, preferred_element_type=jnp.float32)
        + proj_bias
    )
    middle = residual_in + attended
    normed_two, norm_back_two = jax.vjp(layer_norm, middle, gain_two, shift_two)
    normed_two_low = normed_two.astype(jnp.bfloat16)
    pre_act = (
        jnp.einsum("cpd,df->cpf", normed_two_low, w_up, preferred_element_type=jnp.float32)
        + up_bias
    )
    activated, gelu_back = jax.vjp(gelu_exact, pre_act)
    activated_low = activated.astype(jnp.bfloat16)
    output_rows = (
        middle
        + jnp.einsum("cpf,fd->cpd", activated_low, w_down, preferred_element_type=jnp.float32)
        + down_bias
    )
    grad_rows = out_grad.astype(jnp.float32)
    grad_activated = jnp.einsum("cpd,fd->cpf", out_grad, w_down, preferred_element_type=jnp.float32)
    grad_w_down = jnp.einsum(
        "cpf,cpd->fd", activated_low, out_grad, preferred_element_type=jnp.float32
    )
    grad_down_bias = jnp.sum(grad_rows, axis=(0, 1))
    grad_pre_low = gelu_back(grad_activated)[0].astype(jnp.bfloat16)
    grad_w_up = jnp.einsum(
        "cpd,cpf->df", normed_two_low, grad_pre_low, preferred_element_type=jnp.float32
    )
    grad_up_bias = jnp.sum(grad_pre_low.astype(jnp.float32), axis=(0, 1))
    grad_normed_two = jnp.einsum(
        "cpf,df->cpd", grad_pre_low, w_up, preferred_element_type=jnp.float32
    )
    grad_middle_norm, grad_gain_two, grad_shift_two = norm_back_two(grad_normed_two)
    grad_middle = grad_rows + grad_middle_norm
    grad_attended_low = grad_middle.astype(jnp.bfloat16)
    grad_w_proj = jnp.einsum(
        "cpd,cpe->de", context_low, grad_attended_low, preferred_element_type=jnp.float32
    )
    grad_proj_bias = jnp.sum(grad_attended_low.astype(jnp.float32), axis=(0, 1))
    grad_context_low = jnp.einsum(
        "cpe,de->cpd", grad_attended_low, w_proj, preferred_element_type=jnp.float32
    ).astype(jnp.bfloat16)
    grad_context_heads = grad_context_low.reshape(clip_count, row_count, HEADS, head_size)
    probs_again = jnp.exp(scores_of(query_heads, key_rows) - log_total)
    grad_probs = jnp.einsum(
        "cqhd,ckhd->chqk", grad_context_heads, value_rows, preferred_element_type=jnp.float32
    )
    row_terms = jnp.sum(probs_again * grad_probs, axis=-1, keepdims=True)
    grad_scores_low = (probs_again * (grad_probs - row_terms)).astype(jnp.bfloat16)
    grad_queries = (
        jnp.einsum("chqk,ckhd->cqhd", grad_scores_low, key_rows, preferred_element_type=jnp.float32)
        * score_scale
    )
    grad_keys_pad = (
        jnp.einsum(
            "chqk,cqhd->ckhd", grad_scores_low, query_heads, preferred_element_type=jnp.float32
        )
        * score_scale
    )
    grad_values_pad = jnp.einsum(
        "chqk,cqhd->ckhd", probs_low, grad_context_heads, preferred_element_type=jnp.float32
    )
    grad_pair = jnp.concatenate(
        [
            grad_keys_pad.reshape(clip_count, padded_rows, model_width),
            grad_values_pad.reshape(clip_count, padded_rows, model_width),
        ],
        axis=-1,
    )
    grad_pair_own = fold(grad_pair)
    grad_keys_low = grad_pair_own[..., :model_width].astype(jnp.bfloat16)
    grad_values_low = grad_pair_own[..., model_width:].astype(jnp.bfloat16)
    grad_queries_low = grad_queries.reshape(clip_count, row_count, model_width).astype(jnp.bfloat16)
    grad_projected = jnp.concatenate([grad_queries_low, grad_keys_low, grad_values_low], axis=-1)
    grad_w_qkv = jnp.einsum(
        "cpd,cpe->de", normed_low, grad_projected, preferred_element_type=jnp.float32
    )
    grad_query_bias = jnp.sum(grad_queries_low.astype(jnp.float32), axis=(0, 1))
    grad_value_bias = jnp.sum(grad_values_low.astype(jnp.float32), axis=(0, 1))
    grad_normed_one = jnp.einsum(
        "cpe,de->cpd", grad_projected, w_qkv, preferred_element_type=jnp.float32
    )
    grad_input_norm, grad_gain_one, grad_shift_one = norm_back_one(grad_normed_one)
    grad_tokens = (grad_middle + grad_input_norm).astype(jnp.bfloat16)
    grads = (
        grad_w_qkv,
        grad_query_bias,
        grad_value_bias,
        grad_w_proj,
        grad_proj_bias,
        grad_w_up,
        grad_up_bias,
        grad_w_down,
        grad_down_bias,
        grad_gain_one,
        grad_shift_one,
        grad_gain_two,
        grad_shift_two,
    )
    return (output_rows, grad_tokens, grads)


def local(
    tokens,
    out_grad,
    view_masks,
    view_group,
    w_qkv,
    query_bias,
    value_bias,
    w_proj,
    proj_bias,
    w_up,
    up_bias,
    w_down,
    down_bias,
    gain_one,
    shift_one,
    gain_two,
    shift_two,
):
    params = (
        w_qkv,
        query_bias,
        value_bias,
        w_proj,
        proj_bias,
        w_up,
        up_bias,
        w_down,
        down_bias,
        gain_one,
        shift_one,
        gain_two,
        shift_two,
    )
    clip_count, row_count, model_width = tokens.shape
    weight_rows = group_weights(view_masks, view_group)
    frames_dev = row_count // HW
    padded_rows = row_count + 2 * HW
    frame_start = lax.axis_index("frame") * frames_dev
    query_frame = jnp.arange(row_count, dtype=jnp.int32) // HW
    key_frame = jnp.arange(padded_rows, dtype=jnp.int32) // HW - 1
    global_key = frame_start + key_frame
    key_valid = (global_key >= 0) & (global_key < NF)
    allowed = (jnp.abs(query_frame[:, None] - key_frame[None, :]) <= 1) & key_valid[None, :]

    def extend_keys(key_value):
        return with_halo(key_value, (("frame", 1),), HW)

    def fold_grads(grad_pair):
        from_above = from_behind(grad_pair[:, :HW].astype(jnp.bfloat16), "frame", -1).astype(
            jnp.float32
        )
        from_below = from_behind(
            grad_pair[:, row_count + HW :].astype(jnp.bfloat16), "frame", 1
        ).astype(jnp.float32)
        return (
            grad_pair[:, HW : row_count + HW]
            + jnp.pad(from_below, ((0, 0), (0, row_count - HW), (0, 0)))
            + jnp.pad(from_above, ((0, 0), (row_count - HW, 0), (0, 0)))
        )

    output_rows, grad_tokens, grads = layer(
        tokens.astype(jnp.float32), out_grad, params, HW, allowed, extend_keys, fold_grads
    )
    first_sums, second_sums, counts = group_sums(output_rows, weight_rows)
    block_out = output_rows.astype(jnp.bfloat16)
    first_sums, second_sums, counts = lax.psum((first_sums, second_sums, counts), "frame")
    summed = lax.psum(
        (
            grads[0],
            grads[1],
            grads[2],
            grads[3],
            grads[4],
            grads[5],
            grads[6],
            grads[7],
            grads[8],
            grads[9],
            grads[10],
            grads[11],
            grads[12],
        ),
        ("frame", "clip"),
    )
    group_stats = group_moments(first_sums, second_sums, counts)
    return (
        block_out,
        group_stats,
        grad_tokens,
        summed[0],
        summed[1],
        summed[2],
        summed[3],
        summed[4],
        summed[5],
        summed[6],
        summed[7],
        summed[8],
        summed[9],
        summed[10],
        summed[11],
        summed[12],
    )


def solution(mesh):
    in_specs = (
        P("clip", "frame", None),
        P("clip", "frame", None),
        P("clip", None, "frame"),
        P("clip", None),
        P(),
        P(),
        P(),
        P(),
        P(),
        P(),
        P(),
        P(),
        P(),
        P(),
        P(),
        P(),
        P(),
    )
    out_specs = (
        P("clip", "frame", None),
        P("clip", None, None, None),
        P("clip", "frame", None),
        P(),
        P(),
        P(),
        P(),
        P(),
        P(),
        P(),
        P(),
        P(),
        P(),
        P(),
        P(),
        P(),
    )
    return jax.shard_map(local, mesh=mesh, in_specs=in_specs, out_specs=out_specs, check_vma=False)
```

profile of v0, /device:TPU:0, one launch (start us, length us, event | category | flops | bytes accessed | tf_op | source)
XLA Modules:
  0.0 547.9 jit_solution(7656241312504721229)
XLA Ops:
  20.4 7.0 %collective-permute-start = (bf16[4,196,768]{2,0,1:T(4,128)(2,1)}, bf16[4,196,768]{2,0,1:T(4,128)(2,1)}, u32[]{:S(2)}, u32[]{:S(2)}) collective-permute-start(bf16[4,196,768]{2,0,1:T(4,128)(2,1)} %copy.59), channel_id=1, source_target_pairs={{0,8},{8,16},{16,24},{1,9},{9,17},{17,25},{2,10},{10,18},{18,26},{... | collective-permute-start | bytes 3612680 | tf_op jit(solution)/shard_map/ppermute | solution.py:24
  31.9 18.1 %collective-permute-done.1 = bf16[4,196,768]{2,0,1:T(4,128)(2,1)} collective-permute-done((bf16[4,196,768]{2,0,1:T(4,128)(2,1)}, bf16[4,196,768]{2,0,1:T(4,128)(2,1)}, u32[]{:S(2)}, u32[]{:S(2)}) %collective-permute-start.1) | collective-permute-done | bytes 1204256 | tf_op jit(solution)/shard_map/ppermute | solution.py:25
  54.8 2.7 fusion.78
  57.5 4.4 copy.65
  61.9 4.4 copy.63
  66.3 19.3 %fusion = (f32[4,6,392]{2,1,0:T(8,128)S(1)}, f32[4,6,392,784]{3,2,1,0:T(8,128)}) fusion(pred[392,784]{1,0:T(8,128)(4,1)S(1)} %fusion.32, bf16[4,392,6,64]{1,3,2,0:T(8,128)(2,1)} %bitcast.90, bf16[4,784,6,64]{1,3,2,0:T(8,128)(2,1)} %bitcast.87), kind=kOutput, calls=%fused_computation.5 | convolution fusion | flops 966229824 | bytes 33461120 | tf_op jit(solution)/shard_map/cqhd,ckhd->chqk/dot_general | solution.py:108
  85.6 15.3 %exponential_reduce_fusion = f32[4,6,392]{2,1,0:T(8,128)S(1)} fusion(f32[4,6,392,784]{3,2,1,0:T(8,128)} %get-tuple-element.108, f32[4,6,392]{2,1,0:T(8,128)S(1)} %get-tuple-element.107, pred[392,784]{1,0:T(8,128)(4,1)S(1)} %fusion.32), kind=kLoop, calls=%fused_computation.3 | loop fusion | flops 29494080 | bytes 29886080 | tf_op jit(solution)/shard_map/reduce_sum | solution.py:115
  100.9 14.4 %convolution_convert_fusion = bf16[4,6,64,392]{3,2,1,0:T(8,128)(2,1)S(1)} fusion(bf16[4,784,6,64]{1,3,2,0:T(8,128)(2,1)S(1)} %bitcast.93, f32[4,6,392,784]{3,2,1,0:T(8,128)} %get-tuple-element.108, f32[4,6,392]{2,1,0:T(8,128)S(1)} %log_add_fusion, pred[392,784]{1,0:T(8,128)(4,1)S(1)} %fusion.32), kind=kOutput, calls=%fused_computation.83 | convolution fusion | flops 974217216 | bytes 33461120 | tf_op jit(solution)/shard_map/chqk,ckhd->cqhd/dot_general | solution.py:117
  117.4 5.2 fusion.29
  122.7 23.2 %multiply_convert_fusion.1 = (bf16[4,392,1536]{2,1,0:T(8,128)(2,1)}, f32[4,392,1536]{2,1,0:T(8,128)}) fusion(f32[4,392,1536]{2,1,0:T(8,128)S(1)} %get-tuple-element.111, f32[1536]{0:T(1024)S(1)} %copy-done.34, u8[392,1536]{1,0:T(8,128)(4,1)S(1)} %get-tuple-element.65, u8[392,1536]{1,0:T(8,128)(4,1)S(1)} %get-tuple-element.64), kind=kLoop, calls=%fused_computation.20 | loop fusion | flops 170999808 | bytes 25294848 | tf_op jit(solution)/shard_map/convert_element_type | solution.py:133
  145.9 8.6 %convert_reduce_fusion = (f32[1536]{0:T(1024)S(1)}, bf16[4,392,1536]{2,1,0:T(8,128)(2,1)S(1)}) fusion(f32[4,392,1536]{2,1,0:T(8,128)} %get-tuple-element.94, bf16[4,392,384]{2,1,0:T(8,128)(2,1)S(1)} %copy-done.15, bf16[1536,384]{1,0:T(8,128)(2,1)S(1)} %copy-done.43, f32[4,392,1536]{2,1,0:T(8,128)S(1)} %get-tuple-element.111, f32[1536]{0:T(1024)S(1)} %copy-done.34), kind=kOutput, calls=%fused_computation.18 | convolution fusion | flops 1890630144 | bytes 26480640 | tf_op jit(solution)/shard_map/cpd,fd->cpf/dot_general | solution.py:140
  154.5 3.5 multiply_reduce_fusion.1
  166.8 17.1 %fusion.48 = f32[4,6,64,784]{3,2,1,0:T(8,128)} fusion(bf16[4,392,6,64]{1,3,2,0:T(8,128)(2,1)} %bitcast.95, f32[4,6,392,784]{3,2,1,0:T(8,128)} %get-tuple-element.108, f32[4,6,392]{2,1,0:T(8,128)S(1)} %log_add_fusion, pred[392,784]{1,0:T(8,128)(4,1)S(1)} %fusion.32), kind=kOutput, calls=%fused_computation.103 | convolution fusion | flops 973615104 | bytes 35869568 | tf_op jit(solution)/shard_map/chqk,cqhd->ckhd/dot_general | solution.py:180
  183.9 29.3 %multiply_reduce_fusion = (f32[4,6,392]{2,1,0:T(8,128)S(1)}, f32[4,6,392,784]{3,2,1,0:T(8,128)}) fusion(f32[4,6,392,784]{3,2,1,0:T(8,128)} %get-tuple-element.108, f32[4,6,392]{2,1,0:T(8,128)S(1)} %log_add_fusion, pred[392,784]{1,0:T(8,128)(4,1)S(1)} %fusion.32, bf16[4,392,6,64]{1,3,2,0:T(8,128)(2,1)} %bitcast.96, bf16[4,784,6,64]{1,3,2,0:T(8,128)(2,1)} %bitcast.92), kind=kOutput, calls=%fused_computation.1 | convolution fusion | flops 980981568 | bytes 63002240 | tf_op jit(solution)/shard_map/cqhd,ckhd->chqk/dot_general | solution.py:165
  213.2 27.7 %multiply_convert_fusion = bf16[4,6,392,784]{3,2,1,0:T(8,128)(2,1)} fusion(f32[4,6,392,784]{3,2,1,0:T(8,128)} %get-tuple-element.118, f32[4,6,392,784]{3,2,1,0:T(8,128)} %get-tuple-element.108, f32[4,6,392]{2,1,0:T(8,128)S(1)} %get-tuple-element.117, f32[4,6,392]{2,1,0:T(8,128)S(1)} %log_add_fusion, pred[392,784]{1,0:T(8,128)(4,1)S(1)} %fusion.32), kind=kLoop, calls=%fused_computation | loop fusion | flops 44255232 | bytes 74141312 | tf_op jit(solution)/shard_map/convert_element_type | solution.py:169
  240.9 10.1 %convert_reduce_fusion.2 = (f32[6,64]{1,0:T(8,128)S(1)}, bf16[4,6,64,392]{3,2,1,0:T(8,128)(2,1)}) fusion(bf16[4,784,6,64]{1,3,2,0:T(8,128)(2,1)S(1)} %bitcast.88, bf16[4,6,392,784]{3,2,1,0:T(8,128)(2,1)} %multiply_convert_fusion), kind=kOutput, calls=%fused_computation.48 | convolution fusion | flops 946519680 | bytes 18365952 | tf_op jit(solution)/shard_map/chqk,ckhd->cqhd/dot_general | solution.py:171
  251.0 11.1 %broadcast_multiply_fusion = f32[4,6,64,784]{3,2,1,0:T(8,128)} fusion(bf16[4,392,6,64]{1,3,2,0:T(8,128)(2,1)S(1)} %bitcast.91, bf16[4,6,392,784]{3,2,1,0:T(8,128)(2,1)} %multiply_convert_fusion), kind=kOutput, calls=%fused_computation.55 | convolution fusion | flops 945315840 | bytes 20772864 | tf_op jit(solution)/shard_map/chqk,cqhd->ckhd/dot_general | solution.py:175
  262.1 5.9 %copy.70 = f32[4,784,384]{2,1,0:T(8,128)} copy(f32[4,784,384]{1,2,0:T(8,128)} %bitcast.97) | data formatting | bytes 9633792 | tf_op jit(solution)/shard_map/reshape | solution.py:186
  268.0 5.9 %copy.69 = f32[4,784,384]{2,1,0:T(8,128)} copy(f32[4,784,384]{1,2,0:T(8,128)} %bitcast.89) | data formatting | bytes 9633792 | tf_op jit(solution)/shard_map/reshape | solution.py:185
  273.8 4.3 fusion.2
  282.7 26.4 %collective-permute-start.2 = (bf16[4,196,768]{2,0,1:T(4,128)(2,1)}, bf16[4,196,768]{2,0,1:T(4,128)(2,1)}, u32[]{:S(2)}, u32[]{:S(2)}) collective-permute-start(bf16[4,196,768]{2,0,1:T(4,128)(2,1)} %copy.71), channel_id=1, source_target_pairs={{0,8},{8,16},{16,24},{1,9},{9,17},{17,25},{2,10},{10,18},{18,26},{... | collective-permute-start | bytes 3612680 | tf_op jit(solution)/shard_map/ppermute | solution.py:33
  309.1 6.7 %convolution_bitcast_fusion.1 = f32[1536,384]{1,0:T(8,128)} fusion(bf16[4,392,1536]{2,1,0:T(8,128)(2,1)} %get-tuple-element.93, bf16[4,392,384]{2,1,0:T(8,128)(2,1)S(1)} %copy-done.16), kind=kOutput, calls=%fused_computation.53 | convolution fusion | flops 1849688064 | bytes 8380416 | tf_op jit(solution)/shard_map/cpf,cpd->fd/dot_general | solution.py:141
  318.4 3.6 convolution_bitcast_fusion.3
  322.0 7.1 %convolution_bitcast_fusion.2 = f32[384,1536]{1,0:T(8,128)} fusion(bf16[4,392,1536]{2,1,0:T(8,128)(2,1)} %copy-done.14, f32[4,392,384]{2,1,0:T(8,128)} %copy-done.2, f32[384]{0:T(512)S(1)} %copy-done.35, f32[384]{0:T(512)S(1)} %copy-done.32, f32[4,392]{1,0:T(4,128)S(1)} %fusion.56, f32[4,392]{1,0:T(4,128)S(1)} %broadcast_multiply_fusion.1), kind=kOutput, calls=%fused_computation.54 | convolution fusion | flops 1852698624 | bytes 9600256 | tf_op jit(solution)/shard_map/cpd,cpf->df/dot_general | solution.py:146
  329.1 4.6 collective-permute-done.3
  339.3 3.4 convolution_bitcast_fusion
  343.4 7.3 %fusion.80 = (bf16[4,392,384]{2,1,0:T(8,128)(2,1)}, f32[4,392,384]{2,1,0:T(8,128)S(1)}) fusion(f32[384]{0:T(512)S(1)} %copy-done.48, f32[4,392,384]{2,1,0:T(8,128)} %copy-done.2, bf16[4,392,1536]{2,1,0:T(8,128)(2,1)} %get-tuple-element.93, bf16[1536,384]{1,0:T(8,128)(2,1)} %param.28), kind=kOutput, calls=%fused_computation.153 | convolution fusion | flops 1851494400 | bytes 12019200 | tf_op jit(solution)/shard_map/cpf,fd->cpd/dot_general | solution.py:136
  353.5 41.0 %all-reduce.4 = (f32[4,2,384]{2,1,0:T(2,128)S(1)}, f32[4,2]{1,0:T(4,128)S(1)}, f32[4,2,384]{2,1,0:T(2,128)S(1)}) all-reduce(f32[4,2,384]{2,1,0:T(2,128)S(1)} %fusion.26, f32[4,2]{1,0:T(4,128)S(1)} %copy-done.36, f32[4,2,384]{2,1,0:T(2,128)S(1)} %fusion.82), channel_id=1, replica_groups=mesh['frame'=4,'clip'=8] {'frame'}, use_global_device_ids=true, to_apply=%region_9.10 | all-reduce | flops 6152 | bytes 49216 | tf_op jit(solution)/shard_map/psum | solution.py:289
  396.8 4.2 fusion.73
  405.4 40.7 %all-reduce.2 = (f32[384]{0:T(512)}, f32[384]{0:T(512)}, f32[384]{0:T(512)}, f32[1536]{0:T(1024)}, f32[384]{0:T(512)}, /*index=5*/f32[384]{0:T(512)}, f32[384]{0:T(512)}, f32[384]{0:T(512)}, f32[384]{0:T(512)}) all-reduce(f32[384]{0:T(512)S(1)} %reduce_sum.226, ...), channel_id=1, replica_groups=mesh['frame'=4,'clip'=8] {'frame','clip'}, use_global_device_ids=true, to_apply=%region_17.18 | all-reduce | flops 4608 | bytes 36864 | tf_op jit(solution)/shard_map/psum | solution.py:290
  446.1 87.0 %all-reduce.7.cloned.1.call-done = (f32[384,1152]{1,0:T(8,128)}, f32[384,384]{1,0:T(8,128)}, f32[384,1536]{1,0:T(8,128)}, f32[1536,384]{1,0:T(8,128)}) async-done(((f32[384,1152]{1,0:T(8,128)}, f32[384,384]{1,0:T(8,128)}, f32[384,1536]{1,0:T(8,128)}, f32[1536,384]{1,0:T(8,128)}), (f32[384,1152]{1,0:T(8,128)}, f32[384,384]{1,0:T(8,128)}, f32[384,1536]{1,0:T(8,128)}, ...) | async-done | bytes 7077904 | tf_op jit(solution)/shard_map/psum | solution.py:290
  533.1 2.9 copy.84
  (167 shorter events, 60.4 us)
Async XLA Ops:
  7.2 110.1 %copy-start = (bf16[384,1536]{1,0:T(8,128)(2,1)S(1)}, bf16[384,1536]{1,0:T(8,128)(2,1)}, u32[]{:S(2)}) copy-start(bf16[384,1536]{1,0:T(8,128)(2,1)} %param.26) | copy-start | bytes 3538948
  7.2 4.4 copy-start.3
  7.2 4.4 copy-start.37
  7.2 4.4 copy-start.46
  7.2 525.9 %all-reduce.7.cloned.1.call-start = ((), (), s32[]{:S(2)}) async-start(), calls=%async_computation | async-start | bytes 14155776 | tf_op jit(solution)/shard_map/psum | solution.py:290
  7.3 4.4 copy-start.44
  9.1 5.0 copy-start.26
  16.1 11.3 %copy-start.42 = (s32[4,2]{0,1:T(2,128)S(1)}, s32[4,2]{0,1:T(2,128)}, u32[]{:S(2)}) copy-start(s32[4,2]{0,1:T(2,128)} %param.20) | copy-start | bytes 100
  17.6 32.5 %collective-permute-start.1 = (bf16[4,196,768]{2,0,1:T(4,128)(2,1)}, bf16[4,196,768]{2,0,1:T(4,128)(2,1)}, u32[]{:S(2)}, u32[]{:S(2)}) collective-permute-start(bf16[4,196,768]{2,0,1:T(4,128)(2,1)} %copy.60), channel_id=1, source_target_pairs={{8,0},{16,8},{24,16},{9,1},{17,9},{25,17},{10,2},{18,10},{26,18},{... | collective-permute-start | bytes 3612680 | tf_op jit(solution)/shard_map/ppermute | solution.py:25
  18.9 11.2 %copy-start.33 = (s32[4,2,392]{2,1,0:T(2,128)S(1)}, s32[4,2,392]{2,1,0:T(2,128)}, u32[]{:S(2)}) copy-start(s32[4,2,392]{2,1,0:T(2,128)} %param.19) | copy-start | bytes 37636
  20.4 31.5 %collective-permute-start = (bf16[4,196,768]{2,0,1:T(4,128)(2,1)}, bf16[4,196,768]{2,0,1:T(4,128)(2,1)}, u32[]{:S(2)}, u32[]{:S(2)}) collective-permute-start(bf16[4,196,768]{2,0,1:T(4,128)(2,1)} %copy.59), channel_id=1, source_target_pairs={{0,8},{8,16},{16,24},{1,9},{9,17},{17,25},{2,10},{10,18},{18,26},{... | collective-permute-start | bytes 3612680 | tf_op jit(solution)/shard_map/ppermute | solution.py:24
  31.9 21.4 %copy-start.10 = (bf16[4,392,384]{2,1,0:T(8,128)(2,1)S(1)}, bf16[4,392,384]{2,1,0:T(8,128)(2,1)}, u32[]{:S(2)}) copy-start(bf16[4,392,384]{2,1,0:T(8,128)(2,1)} %copy-done.9) | copy-start | bytes 3612676
  31.9 21.4 %copy-start.12 = (bf16[4,392,384]{2,1,0:T(8,128)(2,1)S(1)}, bf16[4,392,384]{2,1,0:T(8,128)(2,1)}, u32[]{:S(2)}) copy-start(bf16[4,392,384]{2,1,0:T(8,128)(2,1)} %copy-done.11) | copy-start | bytes 3612676
  85.6 15.3 %copy-start.8 = (bf16[4,784,384]{1,2,0:T(8,128)(2,1)S(1)}, bf16[4,784,384]{1,2,0:T(8,128)(2,1)}, u32[]{:S(2)}) copy-start(bf16[4,784,384]{1,2,0:T(8,128)(2,1)} %copy.63) | copy-start | bytes 7225348
  100.9 14.4 %copy-start.23 = (bf16[384,384]{1,0:T(8,128)(2,1)S(1)}, bf16[384,384]{1,0:T(8,128)(2,1)}, u32[]{:S(2)}) copy-start(bf16[384,384]{1,0:T(8,128)(2,1)} %param.24) | copy-start | bytes 884740
  100.9 14.4 %copy-start.39 = (f32[384]{0:T(512)S(1)}, f32[384]{0:T(512)}, u32[]{:S(2)}) copy-start(f32[384]{0:T(512)} %param.25) | copy-start | bytes 4612
  116.6 41.5 %copy-start.2 = (f32[4,392,384]{2,1,0:T(8,128)}, f32[4,392,384]{2,1,0:T(8,128)S(1)}, u32[]{:S(2)}) copy-start(f32[4,392,384]{2,1,0:T(8,128)S(1)} %get-tuple-element.110) | copy-start | bytes 7225348
  122.7 23.2 %copy-start.15 = (bf16[4,392,384]{2,1,0:T(8,128)(2,1)S(1)}, bf16[4,392,384]{2,1,0:T(8,128)(2,1)}, u32[]{:S(2)}) copy-start(bf16[4,392,384]{2,1,0:T(8,128)(2,1)} %param.18) | copy-start | bytes 3612676
  122.7 23.2 %copy-start.43 = (bf16[1536,384]{1,0:T(8,128)(2,1)S(1)}, bf16[1536,384]{1,0:T(8,128)(2,1)}, u32[]{:S(2)}) copy-start(bf16[1536,384]{1,0:T(8,128)(2,1)} %param.28) | copy-start | bytes 3538948
  213.2 27.7 %copy-start.4 = (bf16[4,784,384]{1,2,0:T(8,128)(2,1)S(1)}, bf16[4,784,384]{1,2,0:T(8,128)(2,1)}, u32[]{:S(2)}) copy-start(bf16[4,784,384]{1,2,0:T(8,128)(2,1)} %copy.65) | copy-start | bytes 7225348
  240.9 10.1 %copy-start.7 = (bf16[4,392,384]{1,2,0:T(8,128)(2,1)S(1)}, bf16[4,392,384]{1,2,0:T(8,128)(2,1)}, u32[]{:S(2)}) copy-start(bf16[4,392,384]{1,2,0:T(8,128)(2,1)} %copy.64) | copy-start | bytes 3612676
  278.4 30.7 %copy-start.16 = (bf16[4,392,384]{2,1,0:T(8,128)(2,1)S(1)}, bf16[4,392,384]{2,1,0:T(8,128)(2,1)}, u32[]{:S(2)}) copy-start(bf16[4,392,384]{2,1,0:T(8,128)(2,1)} %param.18) | copy-start | bytes 3612676
  281.4 52.3 %collective-permute-start.3 = (bf16[4,196,768]{2,0,1:T(4,128)(2,1)}, bf16[4,196,768]{2,0,1:T(4,128)(2,1)}, u32[]{:S(2)}, u32[]{:S(2)}) collective-permute-start(bf16[4,196,768]{2,0,1:T(4,128)(2,1)} %copy.73), channel_id=1, source_target_pairs={{8,0},{16,8},{24,16},{9,1},{17,9},{25,17},{10,2},{18,10},{26,18},{... | collective-permute-start | bytes 3612680 | tf_op jit(solution)/shard_map/ppermute | solution.py:33
  282.7 52.4 %collective-permute-start.2 = (bf16[4,196,768]{2,0,1:T(4,128)(2,1)}, bf16[4,196,768]{2,0,1:T(4,128)(2,1)}, u32[]{:S(2)}, u32[]{:S(2)}) collective-permute-start(bf16[4,196,768]{2,0,1:T(4,128)(2,1)} %copy.71), channel_id=1, source_target_pairs={{0,8},{8,16},{16,24},{1,9},{9,17},{17,25},{2,10},{10,18},{18,26},{... | collective-permute-start | bytes 3612680 | tf_op jit(solution)/shard_map/ppermute | solution.py:33
  318.4 18.1 %slice-start = ((s8[4816896]{0:T(1024)(128)(4,1)}), s8[4194304]{0:T(1024)(128)(4,1)S(1)}, s32[]{:S(2)}) async-start(s8[4816896]{0:T(1024)(128)(4,1)} %bitcast.83), calls=%async_computation.1 | async-start | bytes 8388608
  318.4 18.1 %slice-start.2 = ((s8[4816896]{0:T(1024)(128)(4,1)}), s8[4194304]{0:T(1024)(128)(4,1)S(1)}, s32[]{:S(2)}) async-start(s8[4816896]{0:T(1024)(128)(4,1)} %bitcast.85), calls=%async_computation.3 | async-start | bytes 8388608
  322.0 14.5 %slice-start.1 = ((s8[4816896]{0:T(1024)(128)(4,1)}), s8[622592]{0:T(1024)(128)(4,1)S(1)}, s32[]{:S(2)}) async-start(s8[4816896]{0:T(1024)(128)(4,1)} %bitcast.83), calls=%async_computation.2 | async-start | bytes 1245184
  322.0 14.5 %slice-start.3 = ((s8[4816896]{0:T(1024)(128)(4,1)}), s8[622592]{0:T(1024)(128)(4,1)S(1)}, s32[]{:S(2)}) async-start(s8[4816896]{0:T(1024)(128)(4,1)} %bitcast.85), calls=%async_computation.4 | async-start | bytes 1245184
  343.4 7.3 %copy-start.25 = (f32[4,2,392]{2,1,0:T(2,128)S(1)}, f32[4,2,392]{2,1,0:T(2,128)}, u32[]{:S(2)}) copy-start(f32[4,2,392]{2,1,0:T(2,128)} %get-tuple-element.115) | copy-start | bytes 37636
  352.1 44.8 %copy-start.45 = (bf16[384,1152]{1,0:T(8,128)(2,1)S(1)}, bf16[384,1152]{1,0:T(8,128)(2,1)}, u32[]{:S(2)}) copy-start(bf16[384,1152]{1,0:T(8,128)(2,1)} %param.21) | copy-start | bytes 2654212
  396.8 4.2 copy-start.29
  536.9 3.9 copy-start.1
  (26 other events, 52.9 us)
Sparse Core Ops, SparseCore 0:
  342.9 190.1 all-reduce.6
where the time goes:
time: 553 us; the launch traced here: 548 us
  matrix products  161 us (29%)
  waiting for transfers between devices  110 us (20%)
  other arithmetic  86.6 us (16%)
  blocking collectives  81.7 us (15%)
  local copies, waits for them, and re-layouts  57.5 us (10%)
  starting transfers between devices  36 us (7%)
  between operations  15.1 us (3%)
    psum x1, waiting for transfers between devices, local(): lax.psum((grads[0], grads[1], grads[2], grads[3], grads[4], grads[5], gra...  87 us
    psum x1, blocking collectives, local(): lax.psum((first_sums, second_sums, counts), 'frame')  41 us
    psum x1, blocking collectives, local(): lax.psum((grads[0], grads[1], grads[2], grads[3], grads[4], grads[5], gra...  40.7 us
    dot_general x1, matrix products, layer(): jnp.einsum('cqhd,ckhd->chqk', grad_context_heads, value_rows, preferred_e...  29.3 us
    ppermute x2, starting transfers between devices, from_behind(): return lax.ppermute(block, axis, route)  27.7 us
    convert_element_type x1, other arithmetic, layer(): (probs_again * (grad_probs - row_terms)).astype(jnp.bfloat16)  27.7 us
    convert_element_type x1, other arithmetic, layer(): activated_low = activated.astype(jnp.bfloat16)  23.2 us
    dot_general x1, matrix products, scores_of(): jnp.einsum('cqhd,ckhd->chqk', query_part, key_part, preferred_element_typ...  19.3 us
  transfers between devices with their start and end apart: 5, of which 4 were waited for; matrix products, arithmetic and copies ran while one was open for 9% of the time, Pallas kernels for 0%

commit v1 on v0

v1 whole, which is shorter than its diff:
```python
import functools

import jax
import jax.numpy as jnp
from jax import lax
from jax.experimental import pallas as pl
from jax.experimental.pallas import tpu as pltpu
from jax.sharding import PartitionSpec as P

HEADS = 6
NF = 8
HW = 196
GROUPS = 2
EPSILON = 1e-06
NEGATIVE = -1e30
MESH = pl.DeviceIdType.MESH
f32 = jnp.float32
bf16 = jnp.bfloat16

D = 384
FF = 1536
KR = 208
QL = 256
QB, VB, PB, UB, DB, G1, S1, G2, S2 = 0, 1, 2, 3, 7, 8, 9, 10, 11
ROWS_A = 2 * FF + D
ROWS_B = 3 * D


def dot(a, b):
    return lax.dot_general(a, b, (((1,), (0,)), ((), ())), preferred_element_type=f32)


def dot_t(a, b):
    return lax.dot_general(a, b, (((1,), (1,)), ((), ())), preferred_element_type=f32)


def iota(shape, dim):
    return lax.broadcasted_iota(jnp.int32, shape, dim)


def low(v):
    return v.astype(bf16)


def wide(v):
    return jnp.concatenate([v, v], axis=1)


def fold(v):
    return v[:, 0:128] + v[:, 128:256]


def eye(n):
    return low(jnp.where(iota((n, n), 0) == iota((n, n), 1), 1.0, 0.0))


def ds(start, size, step):
    return pl.ds(pl.multiple_of(start, step), size)


def when(condition, action):
    if condition is None:
        action()
    else:
        pl.when(condition)(action)


def piece_rows(quarter, nz):
    return next(p for p in range(16, quarter + 1, 16) if quarter % p == 0 and p * nz >= quarter)


class Reduce:
    def __init__(self, rows, g, sb, ag, r2, r3, send, recv, me, nf, nz):
        self.rows, self.g, self.sb, self.ag, self.r2, self.r3 = rows, g, sb, ag, r2, r3
        self.send, self.recv, self.nf, self.nz = send, recv, nf, nz
        self.f, clip = me
        self.core, self.z = lax.rem(clip, 2), lax.div(clip, 2)
        self.half = rows // 2
        self.quarter = self.half // nf
        self.piece = piece_rows(self.quarter, nz)
        self.owners = self.quarter // self.piece
        self.base = self.core * self.half
        self.qbase = self.base + self.f * self.quarter
        self.pbase = self.qbase + self.z * self.piece

    def at(self, start, size, ref=None):
        return (self.ag if ref is None else ref).at[ds(start, size, 16), :]

    def copies(self, stage):
        nf, nz, out = self.nf, self.nz, []
        if stage == 1:
            o = self.at((1 - self.core) * self.half, self.half, self.sb)
            out = [(o, o, (self.f, self.z * 2 + 1 - self.core), 0, None, None)]
        if stage in (2, 5):
            for k in range(1, nf):
                t = lax.rem(self.f + k, nf)
                dev = (t, self.z * 2 + self.core)
                if stage == 2:
                    src = self.at(self.base + t * self.quarter, self.quarter, self.sb)
                    out.append((src, self.r2.at[k - 1], dev, k, None, None))
                else:
                    src = self.at(self.qbase, self.quarter)
                    out.append((src, src, dev, nf + 2 * nz + k - 3, None, None))
        if stage in (3, 4):
            mine = None if self.owners == nz else self.z < self.owners
            for k in range(1, nz):
                t = lax.rem(self.z + k, nz)
                s = lax.rem(self.z + nz - k, nz)
                dev = (self.f, t * 2 + self.core)
                theirs = None if self.owners == nz else t < self.owners
                comes = None if self.owners == nz else s < self.owners
                if stage == 3:
                    src = self.at(self.qbase + t * self.piece, self.piece, self.sb)
                    out.append((src, self.r3.at[k - 1], dev, nf + k - 1, theirs, mine))
                else:
                    src = self.at(self.pbase, self.piece)
                    out.append((src, src, dev, nf + nz + k - 2, mine, comes))
        if stage == 6:
            s = self.at(self.base, self.half)
            dev = (self.f, self.z * 2 + 1 - self.core)
            out = [(s, s, dev, 2 * nf + 2 * nz - 3, None, None)]
        return [
            (
                pltpu.make_async_remote_copy(
                    src_ref=s,
                    dst_ref=d,
                    send_sem=self.send.at[i],
                    recv_sem=self.recv.at[i],
                    device_id=dev,
                    device_id_type=MESH,
                ),
                sent,
                comes,
            )
            for s, d, dev, i, sent, comes in out
        ]

    def start(self, stage):
        for c, sent, _ in self.copies(stage):
            when(sent, c.start)

    def wait(self, stage):
        for c, sent, comes in self.copies(stage):
            when(comes, c.wait_recv)
            when(sent, c.wait_send)

    def step(self, stage):
        if stage > 1:
            self.wait(stage - 1)
        g, sb, ag = self.g, self.sb, self.ag
        if stage == 1:
            rows = ds((1 - self.core) * self.half, self.half, 16)
            sb[rows, :] = low(g[rows, :])
        if stage == 2:
            rows = ds(self.base, self.half, 16)
            total = g[rows, :] + sb[rows, :].astype(f32)
            g[rows, :] = total
            sb[rows, :] = low(total)
        if stage == 3:
            rows = ds(self.qbase, self.quarter, 16)
            total = g[rows, :]
            for k in range(self.nf - 1):
                total += self.r2[k].astype(f32)
            g[rows, :] = total
            sb[rows, :] = low(total)
        if stage == 4:

            def sum_piece():
                rows = ds(self.pbase, self.piece, 16)
                total = g[rows, :]
                for k in range(self.nz - 1):
                    total += self.r3[k].astype(f32)
                ag[rows, :] = low(total)

            when(None if self.owners == self.nz else self.z < self.owners, sum_piece)
        if stage < 7:
            self.start(stage)

    @staticmethod
    def count(nf, nz):
        return 2 * nf + 2 * nz - 2


def body(
    nf,
    nz,
    rows_a,
    rows_b,
    tok,
    og,
    masks,
    grp,
    wqkv,
    wp,
    wu,
    wd,
    vecs,
    bout,
    stats,
    gtok,
    out_a,
    out_b,
    wqkvT,
    wpT,
    wuT,
    wdT,
    cb,
    TI,
    OS,
    xs,
    ys,
    mw,
    XT,
    n1T,
    NR,
    QT,
    KT,
    VT,
    Kr,
    Vr,
    ctxT,
    n2T,
    actT,
    dpreT,
    gattT,
    dyR,
    dOT,
    ST,
    dmid,
    DQ,
    DK,
    DV,
    acc,
    SP,
    SPr,
    GA,
    GB,
    SB,
    agA,
    agB,
    r2A,
    r3A,
    r2B,
    r3B,
    nr_send,
    nr_recv,
    do_send,
    do_recv,
    st_send,
    st_recv,
    sp_send,
    sp_recv,
    sendA,
    recvA,
    sendB,
    recvB,
    out_sem,
    in_sem,
    row_sem,
):
    clips = tok.shape[0]
    rows = tok.shape[1]
    me_f = lax.axis_index("frame")
    me_c = lax.axis_index("clip")
    core, zi = lax.rem(me_c, 2), lax.div(me_c, 2)
    first, last = me_f == 0, me_f == nf - 1

    def fetch(ref, k, c):
        return pltpu.make_async_copy(ref.at[c], TI.at[c], in_sem.at[k, c])

    def put(n, ref, c):
        slot = lax.rem(n, 2)
        cp = pltpu.make_async_copy(OS.at[slot], ref.at[c], row_sem.at[slot])
        pl.when(n >= 2)(cp.wait)
        OS[slot] = low(ys[0:rows, :])
        cp.start()

    for c in range(clips):
        fetch(tok, 0, c).start()

    NR[...] = jnp.zeros(NR.shape, bf16)
    for c in range(clips):
        for s in (0, 3):
            dOT[c * 4 + s] = jnp.zeros(dOT.shape[1:], bf16)
            ST[c * 4 + s] = jnp.where(iota((3, 8, QL), 1) < 2, 1e30, 0.0)

    barrier = pltpu.get_barrier_semaphore()
    peers = [(lax.rem(me_f + k, nf), me_c) for k in range(1, nf)]
    peers.append((me_f, zi * 2 + 1 - core))
    peers += [(me_f, lax.rem(zi + k, nz) * 2 + core) for k in range(1, nz)]
    for peer in peers:
        pl.semaphore_signal(barrier, inc=1, device_id=peer, device_id_type=MESH)

    def halo(src, dst, send, recv, to_right):
        return pltpu.make_async_remote_copy(
            src_ref=src,
            dst_ref=dst,
            send_sem=send,
            recv_sem=recv,
            device_id=((me_f + 1) if to_right else (me_f - 1), me_c),
            device_id_type=MESH,
        )

    def nr_copy(c, right):
        i, o, k = (2, 0, 0) if right else (1, 3, 1)
        return halo(
            NR.at[c * 4 + i, pl.ds(0, KR)],
            NR.at[c * 4 + o, pl.ds(0, KR)],
            nr_send.at[c, k],
            nr_recv.at[c, k],
            right,
        )

    def do_copies(c, right):
        i, o, k = (2, 0, 0) if right else (1, 3, 1)
        return (
            halo(
                dOT.at[c * 4 + i], dOT.at[c * 4 + o], do_send.at[c, k], do_recv.at[c, k], right
            ),
            halo(ST.at[c * 4 + i], ST.at[c * 4 + o], st_send.at[c, k], st_recv.at[c, k], right),
        )

    def each_side(start, make):
        for right, here, there in ((True, last, first), (False, first, last)):

            @pl.when(jnp.logical_not(here))
            def _():
                for cp in make(right):
                    if start:
                        cp.start()
                    else:
                        cp.wait_send()

            if not start:

                @pl.when(jnp.logical_not(there))
                def _():
                    for cp in make(right):
                        cp.wait_recv()

    xs[...] = jnp.zeros(xs.shape, f32)
    mw[...] = jnp.zeros(mw.shape, f32)
    one_d = eye(D)
    one_q = eye(QL)

    def column(i):
        return wide(cb[i])

    for i in range(12):
        cb[i] = jnp.transpose(jnp.broadcast_to(vecs[i : i + 1, :], (128, D)))
    n1T[...] = jnp.ones(n1T.shape, bf16)
    n2T[...] = jnp.ones(n2T.shape, bf16)
    ctxT[...] = jnp.ones(ctxT.shape, bf16)
    pl.semaphore_wait(barrier, len(peers))

    def frame_rows(f):
        v = xs[pl.ds(HW * f, KR), :]
        tail = jnp.where(iota((16, D), 0) < HW - (KR - 16), v[KR - 16 :], 0.0)
        return low(jnp.concatenate([v[: KR - 16], tail, jnp.zeros((QL - KR, D), f32)], axis=0))

    def norm_one(c, _):
        fetch(tok, 0, c).wait()
        xs[0:rows, :] = TI[c].astype(f32)
        fetch(og, 1, c).start()
        for f in range(2):
            xT = dot_t(one_d, frame_rows(f))
            XT[c * 2 + f] = low(xT)
            cent = xT - jnp.sum(xT, axis=0, keepdims=True) * (1.0 / D)
            var = jnp.sum(cent * cent, axis=0, keepdims=True) * (1.0 / D)
            nT = low(cent * lax.rsqrt(var + EPSILON) * column(G1) + column(S1))
            n1T[c, 0:D, f * QL : (f + 1) * QL] = nT
            NR[c * 4 + f + 1, 0:KR, :] = low(dot_t(one_q[0:KR], nT))
        each_side(True, lambda right: (nr_copy(c, right),))
        return 0

    lax.fori_loop(0, clips, norm_one, 0)

    for j in range(3):
        wqkvT[j * D : (j + 1) * D, :] = low(dot_t(one_d, wqkv[:, j * D : (j + 1) * D]))
    wpT[...] = low(dot_t(one_d, wp[...]))
    for j in range(4):
        wuT[j * D : (j + 1) * D, :] = low(dot_t(one_d, wu[:, j * D : (j + 1) * D]))
        wdT[:, j * D : (j + 1) * D] = low(dot_t(one_d, wd[j * D : (j + 1) * D, :]))
    for r in (GA, GB, acc):
        r[...] = jnp.zeros(r.shape, f32)
    DK[...] = jnp.zeros(DK.shape, bf16)
    KT[...] = jnp.zeros(KT.shape, bf16)
    DV[...] = jnp.zeros(DV.shape, bf16)

    before_bias = jnp.where(first, NEGATIVE, 0.0).astype(f32)
    after_bias = jnp.where(last, NEGATIVE, 0.0).astype(f32)
    z64 = jnp.zeros((64, QL), bf16)
    zpad = jnp.zeros((QL - KR, QL), bf16)

    def split_heads(v):
        return (
            jnp.concatenate([v[0:64], z64], axis=0),
            jnp.concatenate([z64, v[64:128]], axis=0),
        )

    def project(c, s):
        i = c * 4 + s
        qT = low(low(dot_t(wqkvT[0:D, :], NR[i]) + column(QB)) * 0.125)
        vT = low(dot_t(wqkvT[2 * D :, :], NR[i]) + column(VB))
        k = low(dot(NR[i, 0:KR], wqkv[:, D : 2 * D]))
        v = low(dot(NR[i, 0:KR], wqkv[:, 2 * D :]) + vecs[VB : VB + 1, :])
        for p in range(3):
            sl = slice(p * 128, (p + 1) * 128)
            QT[i, p] = qT[sl]
            VT[s, p] = vT[sl]
            Kr[i, p] = k[:, sl]
            Vr[i, p] = v[:, sl]

    def forward_pair(c, p):
        for f in range(2):
            i = c * 4 + f + 1
            out = []
            for hh, qm in enumerate(split_heads(QT[i, p])):
                parts = []
                for j in range(3):
                    s = dot(Kr[c * 4 + f + j, p], qm)
                    tail = jnp.where(iota((16, QL), 0) < HW - (KR - 16), s[KR - 16 :], NEGATIVE)
                    s = jnp.concatenate([s[: KR - 16], tail], axis=0)
                    if f + j == 0:
                        s = s + before_bias
                    if f + j == 3:
                        s = s + after_bias
                    parts.append(s)
                top = functools.reduce(
                    jnp.maximum, [jnp.max(s, axis=0, keepdims=True) for s in parts]
                )
                total = jnp.zeros((1, QL), f32)
                ctx = jnp.zeros((64, QL), f32)
                for j in range(3):
                    e = jnp.exp(parts[j] - top)
                    total += jnp.sum(e, axis=0, keepdims=True)
                    e = jnp.concatenate([low(e), zpad], axis=0)
                    ctx += dot(VT[f + j, p, hh * 64 : hh * 64 + 64, :], e)
                out.append(ctx / total)
                ST[i, p, hh : hh + 1, :] = top + jnp.log(total)
            ctxT[ds(p * 128, 128, 128), f * QL : (f + 1) * QL] = low(
                jnp.concatenate(out, axis=0)
            )

    def gelu_parts(v):
        z = jnp.abs(v) * 0.7071067811865476
        t = 1.0 / (1.0 + 0.3275911 * z)
        e = jnp.exp(v * v * -0.5)
        poly = 0.5 * 1.061405429
        poly = poly * t + 0.5 * -1.453152027
        poly = poly * t + 0.5 * 1.421413741
        poly = poly * t + 0.5 * -0.284496736
        poly = poly * t + 0.5 * 0.254829592
        h = poly * t * e
        phi = jnp.where(v >= 0, 1.0 - h, h)
        return phi, v * (e * 0.3989422804014327)

    def feed_forward(c, f):
        b = c * 2 + f
        lanes = slice(f * QL, (f + 1) * QL)
        xT = XT[b].astype(f32)
        mid = xT + (dot(wpT[...], ctxT[0:D, lanes]) + column(PB))
        cent = mid - jnp.sum(mid, axis=0, keepdims=True) * (1.0 / D)
        var = jnp.sum(cent * cent, axis=0, keepdims=True) * (1.0 / D)
        r = lax.rsqrt(var + EPSILON)
        xh = cent * r
        nT = low(xh * column(G2) + column(S2))
        n2T[0:D, lanes] = nT
        dy = frame_rows(f)
        dyR[lanes, :] = dy
        dyT = dot_t(one_d, dy)
        dyl = low(dyT)
        outT = mid + column(DB)
        dn = jnp.zeros((D, QL), f32)
        for j in range(4):
            sl = slice(j * D, (j + 1) * D)
            pre = dot(wuT[sl, :], nT) + column(UB + j)
            phi, slope = gelu_parts(pre)
            act = low(pre * phi)
            actT[sl, lanes] = act
            dpre = low(dot(wd[sl, :], dyl) * (phi + slope))
            dpreT[sl, lanes] = dpre
            outT += dot(wdT[:, sl], act)
            dn += dot(wu[:, sl], dpre)
        outl = low(outT)
        ys[pl.ds(HW * f, KR), :] = dot_t(one_q[0:KR], outl)
        sq = outT * outT
        out2 = low(outT - outl.astype(f32))
        sql = low(sq)
        sq2 = low(sq - sql.astype(f32))
        m = mw[...]
        if f == 1:
            m = pltpu.roll(m, 2 * QL - HW, 1)
        m = jnp.where(iota((8, QL), 1) < HW, m[:, 0:QL], 0.0)
        w = []
        for g in range(GROUPS):
            w.append(
                sum(
                    m[v : v + 1, :] * jnp.where(grp[c, v] == g, 1.0, 0.0).astype(f32)
                    for v in range(2)
                )
            )
        row = iota((16, QL), 0)

        def place(k):
            return jnp.where(row == k, w[0], jnp.where(row == k + 1, w[1], 0.0))

        w1, w2 = low(place(0)), low(place(2))
        cnt = jnp.sum(place(4), axis=1, keepdims=True)
        sums = dot_t(w1, outl) + dot_t(w1, out2) + dot_t(w2, sql) + dot_t(w2, sq2) + cnt
        if f == 0:
            SP[c] = sums[0:8]
        else:
            SP[c] = SP[c] + sums[0:8]
        acc[0] += fold(dn * xh)
        acc[1] += fold(dn)
        gg = dn * column(G2)
        m1 = jnp.sum(gg, axis=0, keepdims=True) * (1.0 / D)
        m2 = jnp.sum(gg * xh, axis=0, keepdims=True) * (1.0 / D)
        gm = dyT + r * (gg - m1 - xh * m2)
        dmid[b] = gm
        ga = low(gm)
        gattT[:, lanes] = ga
        gc = low(dot(wp[...], ga))
        i = c * 4 + f + 1
        prod = gc.astype(f32) * ctxT[0:D, lanes].astype(f32)
        for h in range(HEADS):
            ST[i, h // 2, 2 + h % 2 : 3 + h % 2, :] = jnp.sum(
                prod[h * 64 : h * 64 + 64], axis=0, keepdims=True
            )
        for p in range(3):
            dOT[i, p] = gc[p * 128 : (p + 1) * 128]

    def weight_grads():
        def chunk(j, _):
            at = ds(j * D, D, D)
            GA[at, :] += dot(actT[at, :], dyR[...])
            g = dot_t(n2T[...], dpreT[at, :])
            GA[ds(FF + j * D, D, D), :] += g[0:D]
            GA[pl.ds(ROWS_A + j, 1), :] += g[D : D + 1]
            return 0

        lax.fori_loop(0, 4, chunk, 0)
        g = dot_t(ctxT[...], gattT[...])
        GA[2 * FF : 2 * FF + D, :] += g[0:D]
        GA[ROWS_A + 4 : ROWS_A + 5, :] += g[D : D + 1]
        GA[ROWS_A + 5 : ROWS_A + 6, :] += dot(n2T[D : D + 16, :], dyR[...])[0:1]

    def front(c, _):
        project(c, 1)
        project(c, 2)
        each_side(False, lambda right: (nr_copy(c, right),))
        project(c, 0)
        project(c, 3)

        def pair(p, _):
            forward_pair(c, p)
            return 0

        lax.fori_loop(0, 3, pair, 0)
        fetch(og, 1, c).wait()
        xs[0:rows, :] = TI[c].astype(f32)
        mw[0:2, 0:rows] = masks[c].astype(f32)
        for f in range(2):
            feed_forward(c, f)
        each_side(True, lambda right: do_copies(c, right))
        put(c, bout, c)
        weight_grads()
        return 0

    lax.fori_loop(0, clips, front, 0)

    def gather_rows(ref, row, k):
        ref[row : row + 1, :] = jnp.sum(jnp.transpose(acc[k]), axis=0, keepdims=True)

    gather_rows(GA, ROWS_A + 6, 0)
    gather_rows(GA, ROWS_A + 7, 1)

    me = (me_f, me_c)
    redA = Reduce(rows_a, GA, SB, agA, r2A, r3A, sendA, recvA, me, nf, nz)
    redB = Reduce(rows_b, GB, SB, agB, r2B, r3B, sendB, recvB, me, nf, nz)

    def sp_copies():
        return [
            pltpu.make_async_remote_copy(
                src_ref=SP,
                dst_ref=SPr.at[k - 1],
                send_sem=sp_send.at[k - 1],
                recv_sem=sp_recv.at[k - 1],
                device_id=(lax.rem(me_f + k, nf), me_c),
                device_id_type=MESH,
            )
            for k in range(1, nf)
        ]

    for cp in sp_copies():
        cp.start()

    def back_block(i, g, p, qms, doms, own):
        out_q, gk, gv = [], jnp.zeros((KR, 128), f32), jnp.zeros((KR, 128), f32)
        for hh in range(2):
            lse = ST[i, p, hh : hh + 1, :]
            delta = ST[i, p, 2 + hh : 3 + hh, :]
            s = dot(Kr[g, p], qms[hh])
            pr = jnp.exp(s - lse)
            if own[2] is not None:
                pr = pr * own[2]
            tail = jnp.where(iota((16, QL), 0) < HW - (KR - 16), pr[KR - 16 :], 0.0)
            pr = jnp.concatenate([pr[: KR - 16], tail], axis=0)
            dp = dot(Vr[g, p], doms[hh])
            dsc = low(pr * (dp - delta))
            if own[1]:
                gv += dot_t(low(pr), doms[hh])
                gk += dot_t(dsc, qms[hh])
            if own[0]:
                dsp = jnp.concatenate([dsc, zpad], axis=0)
                out_q.append(dot(KT[lax.rem(g, 4), p, hh * 64 : hh * 64 + 64, :], dsp))
        return out_q, gk, gv

    has_before = jnp.where(first, 0.0, 1.0).astype(f32)
    has_after = jnp.where(last, 0.0, 1.0).astype(f32)

    def back_pair(c, p):
        gks = [jnp.zeros((KR, 128), f32)] * 2
        gvs = [jnp.zeros((KR, 128), f32)] * 2
        for q in (1, 2, 0, 3):
            i = c * 4 + q
            qms = split_heads(QT[i, p])
            doms = split_heads(dOT[i, p])
            keys = {1: (0, 1, 2), 2: (1, 2, 3), 0: (1,), 3: (2,)}[q]
            total = [jnp.zeros((64, QL), f32)] * 2
            for g in keys:
                keep = {0: has_before, 3: has_after}.get(g)
                own = (q in (1, 2), g in (1, 2), keep)
                dq, gk, gv = back_block(i, c * 4 + g, p, qms, doms, own)
                if own[0]:
                    total = [total[0] + dq[0], total[1] + dq[1]]
                if own[1]:
                    gks[g - 1] = gks[g - 1] + gk
                    gvs[g - 1] = gvs[g - 1] + gv
            if q in (1, 2):
                DQ[q - 1, ds(p * 128, 128, 128), :] = low(
                    jnp.concatenate(total, axis=0) * 0.125
                )
        for f in range(2):
            DK[f, p, 0:KR, :] = low(gks[f])
            DV[f, p, 0:KR, :] = low(gvs[f])

    redA.step(1)

    def back(c, _):
        each_side(False, lambda right: do_copies(c, right))
        for g in range(4):
            for p in range(3):
                KT[g, p, :, 0:KR] = low(dot_t(one_q[0:128, 0:128], Kr[c * 4 + g, p]))

        def pair(p, _):
            back_pair(c, p)
            it = c * 3 + p
            for stage, when in ((2, 1), (3, 4), (4, 6), (5, 8), (6, 10)):

                @pl.when(it == when)
                def _():
                    redA.step(stage)

            return 0

        lax.fori_loop(0, 3, pair, 0)
        dqs, dks, dvs = [], [], []
        for f in range(2):
            b = c * 2 + f
            dq = DQ[f]
            dk = jnp.concatenate([DK[f, p] for p in range(3)], axis=1)
            dv = jnp.concatenate([DV[f, p] for p in range(3)], axis=1)
            dqs.append(dq)
            dks.append(dk)
            dvs.append(dv)
            dn = dot(wqkv[:, 0:D], dq) + dot_t(wqkv[:, D : 2 * D], dk)
            dn += dot_t(wqkv[:, 2 * D :], dv)
            xT = XT[b].astype(f32)
            cent = xT - jnp.sum(xT, axis=0, keepdims=True) * (1.0 / D)
            var = jnp.sum(cent * cent, axis=0, keepdims=True) * (1.0 / D)
            r = lax.rsqrt(var + EPSILON)
            xh = cent * r
            acc[2] += fold(dn * xh)
            acc[3] += fold(dn)
            gg = dn * column(G1)
            m1 = jnp.sum(gg, axis=0, keepdims=True) * (1.0 / D)
            m2 = jnp.sum(gg * xh, axis=0, keepdims=True) * (1.0 / D)
            gT = low(dmid[b] + r * (gg - m1 - xh * m2))
            ys[pl.ds(HW * f, KR), :] = dot_t(one_q[0:KR], gT)
        put(clips + c, gtok, c)
        n1 = n1T[c]
        g = dot_t(n1, jnp.concatenate(dqs, axis=1))
        GB[0:D, :] += g[0:D]
        GB[ROWS_B : ROWS_B + 1, :] += g[D : D + 1]
        GB[D : 2 * D, :] += dot(n1[0:D], jnp.concatenate(dks, axis=0))
        g = dot(n1, jnp.concatenate(dvs, axis=0))
        GB[2 * D : 3 * D, :] += g[0:D]
        GB[ROWS_B + 1 : ROWS_B + 2, :] += g[D : D + 1]
        return 0

    lax.fori_loop(0, clips, back, 0)
    gather_rows(GB, ROWS_B + 2, 2)
    gather_rows(GB, ROWS_B + 3, 3)

    redA.step(7)
    redB.step(1)
    copy_a = pltpu.make_async_copy(agA, out_a, out_sem.at[0])
    copy_a.start()
    for cp in sp_copies():
        cp.wait()
    for c in range(clips):
        t = SP[c] + sum(SPr[k, c] for k in range(nf - 1))
        inv = 1.0 / jnp.maximum(t[4:6], 1.0)
        mean = t[0:2] * inv
        var = t[2:4] * inv - mean * mean
        stats[c, 0:1, :] = mean[0:1]
        stats[c, 1:2, :] = var[0:1]
        stats[c, 2:3, :] = mean[1:2]
        stats[c, 3:4, :] = var[1:2]
    for stage in range(2, 8):
        redB.step(stage)
    copy_b = pltpu.make_async_copy(agB, out_b, out_sem.at[1])
    copy_b.start()
    for slot in range(2):
        pltpu.make_async_copy(OS.at[slot], gtok.at[0], row_sem.at[slot]).wait()
    copy_a.wait()
    copy_b.wait()


def local(nf, nz, tokens, out_grad, view_masks, view_group, *params):
    w_qkv, query_bias, value_bias, w_proj, proj_bias, w_up, up_bias, w_down = params[:8]
    down_bias, gain_one, shift_one, gain_two, shift_two = params[8:]
    clips, rows, width = tokens.shape
    unit = 512
    rows_a = -(-(ROWS_A + 8) // unit) * unit
    rows_b = -(-(ROWS_B + 4) // unit) * unit
    vecs = jnp.concatenate(
        [
            query_bias,
            value_bias,
            proj_bias,
            up_bias,
            down_bias,
            gain_one,
            shift_one,
            gain_two,
            shift_two,
        ]
    ).reshape(12, D)
    vmem = pl.BlockSpec(memory_space=pltpu.VMEM)
    hbm = pl.BlockSpec(memory_space=pl.ANY)
    sems = pltpu.SemaphoreType.DMA
    n_red = Reduce.count(nf, nz)
    bout, stats, gtok, out_a, out_b = pl.pallas_call(
        functools.partial(body, nf, nz, rows_a, rows_b),
        out_shape=(
            jax.ShapeDtypeStruct((clips, rows, D), bf16),
            jax.ShapeDtypeStruct((clips, 4, D), f32),
            jax.ShapeDtypeStruct((clips, rows, D), bf16),
            jax.ShapeDtypeStruct((rows_a, D), bf16),
            jax.ShapeDtypeStruct((rows_b, D), bf16),
        ),
        in_specs=[hbm, hbm, vmem, pl.BlockSpec(memory_space=pltpu.SMEM)] + [vmem] * 5,
        out_specs=(hbm, vmem, hbm, hbm, hbm),
        scratch_shapes=[
            pltpu.VMEM((3 * D, D), bf16),
            pltpu.VMEM((D, D), bf16),
            pltpu.VMEM((FF, D), bf16),
            pltpu.VMEM((D, FF), bf16),
            pltpu.VMEM((12, D, 128), f32),
            pltpu.VMEM((clips, rows, D), bf16),
            pltpu.VMEM((2, rows, D), bf16),
            pltpu.VMEM((416, D), f32),
            pltpu.VMEM((416, D), f32),
            pltpu.VMEM((8, 2 * QL), f32),
            pltpu.VMEM((clips * 2, D, QL), bf16),
            pltpu.VMEM((clips, D + 16, 2 * QL), bf16),
            pltpu.VMEM((clips * 4, QL, D), bf16),
            pltpu.VMEM((clips * 4, 3, 128, QL), bf16),
            pltpu.VMEM((4, 3, 128, QL), bf16),
            pltpu.VMEM((4, 3, 128, QL), bf16),
            pltpu.VMEM((clips * 4, 3, KR, 128), bf16),
            pltpu.VMEM((clips * 4, 3, KR, 128), bf16),
            pltpu.VMEM((D + 16, 2 * QL), bf16),
            pltpu.VMEM((D + 16, 2 * QL), bf16),
            pltpu.VMEM((FF, 2 * QL), bf16),
            pltpu.VMEM((FF, 2 * QL), bf16),
            pltpu.VMEM((D, 2 * QL), bf16),
            pltpu.VMEM((2 * QL, D), bf16),
            pltpu.VMEM((clips * 4, 3, 128, QL), bf16),
            pltpu.VMEM((clips * 4, 3, 8, QL), f32),
            pltpu.VMEM((clips * 2, D, QL), f32),
            pltpu.VMEM((2, D, QL), bf16),
            pltpu.VMEM((2, 3, QL, 128), bf16),
            pltpu.VMEM((2, 3, QL, 128), bf16),
            pltpu.VMEM((4, D, 128), f32),
            pltpu.VMEM((clips, 8, D), f32),
            pltpu.VMEM((nf - 1, clips, 8, D), f32),
            pltpu.VMEM((rows_a, D), f32),
            pltpu.VMEM((rows_b, D), f32),
            pltpu.VMEM((max(rows_a, rows_b), D), bf16),
            pltpu.VMEM((rows_a, D), bf16),
            pltpu.VMEM((rows_b, D), bf16),
            pltpu.VMEM((nf - 1, rows_a // (2 * nf), D), bf16),
            pltpu.VMEM((nz - 1, piece_rows(rows_a // (2 * nf), nz), D), bf16),
            pltpu.VMEM((nf - 1, rows_b // (2 * nf), D), bf16),
            pltpu.VMEM((nz - 1, piece_rows(rows_b // (2 * nf), nz), D), bf16),
            sems((clips, 2)),
            sems((clips, 2)),
            sems((clips, 2)),
            sems((clips, 2)),
            sems((clips, 2)),
            sems((clips, 2)),
            sems((nf - 1,)),
            sems((nf - 1,)),
            sems((n_red,)),
            sems((n_red,)),
            sems((n_red,)),
            sems((n_red,)),
            sems((2,)),
            sems((2, clips)),
            sems((2,)),
        ],
        compiler_params=pltpu.CompilerParams(
            collective_id=0, has_side_effects=True, vmem_limit_bytes=64 * 1024 * 1024 - 65536
        ),
    )(tokens, out_grad, view_masks, view_group, w_qkv, w_proj, w_up, w_down, vecs)

    def side(block, n):
        return block.reshape(n, D, D).transpose(1, 0, 2).reshape(D, n * D).astype(f32)

    def vec(a, row, n=1):
        return a[row : row + n].reshape(n * D).astype(f32)

    return (
        bout,
        stats.reshape(clips, GROUPS, 2, D),
        gtok,
        side(out_b[0 : 3 * D], 3),
        vec(out_b, ROWS_B),
        vec(out_b, ROWS_B + 1),
        out_a[2 * FF : 2 * FF + D].astype(f32),
        vec(out_a, ROWS_A + 4),
        side(out_a[FF : 2 * FF], 4),
        vec(out_a, ROWS_A, 4),
        out_a[0:FF].astype(f32),
        vec(out_a, ROWS_A + 5),
        vec(out_b, ROWS_B + 2),
        vec(out_b, ROWS_B + 3),
        vec(out_a, ROWS_A + 6),
        vec(out_a, ROWS_A + 7),
    )


def solution(mesh):
    row = P("clip", "frame", None)
    in_specs = (row, row, P("clip", None, "frame"), P("clip", None)) + (P(),) * 13
    out_specs = (row, P("clip", None, None, None), row) + (P(),) * 13
    step = functools.partial(local, mesh.shape["frame"], mesh.shape["clip"] // 2)
    return jax.shard_map(step, mesh=mesh, in_specs=in_specs, out_specs=out_specs, check_vma=False)
```

time: 553 us -> 210 us (0.38)
  Pallas kernels: 0 us -> 182 us
  matrix products: 161 us -> 0 us
  waiting for transfers between devices: 110 us -> 0 us
  blocking collectives: 81.7 us -> 0 us
  other arithmetic: 86.6 us -> 7.44 us
  local copies, waits for them, and re-layouts: 57.5 us -> 19.7 us
  starting transfers between devices: 36 us -> 0 us
  between operations: 15.1 us -> 0.7 us
    pallas_call x0 -> x1, Pallas kernels: none -> 182 us  [local(): pl.pallas_call(functools.partial(body, nf, nz, rows_a, rows_b), out_shape...]
    dot_general x21 -> x0, matrix products: 161 us -> none  [the longest x1 29.3 us: layer(): jnp.einsum('cqhd,ckhd->chqk', grad_context_heads, value_rows, preferred_e...]
    psum x1 -> x0, waiting for transfers between devices: 87 us -> none  [local(): lax.psum((grads[0], grads[1], grads[2], grads[3], grads[4], grads[5], gra...]
    psum x2 -> x0, blocking collectives: 81.7 us -> none  [the longest x1 41 us: local(): lax.psum((first_sums, second_sums, counts), 'frame')]
    convert_element_type x3 -> x4, other arithmetic: 52.3 us -> 7.29 us  [the longest x1 3.28 us: local(): out_a[0:FF].astype(f32)]
    ppermute x4 -> x0, starting transfers between devices: 36 us -> none  [the longest x2 27.7 us: from_behind(): return lax.ppermute(block, axis, route)]
    reduce_sum x9 -> x0, other arithmetic: 26.4 us -> none  [the longest x1 15.3 us: layer(): jnp.sum(jnp.exp(scores - top_score), axis=-1, keepdims=True)]
    ppermute x4 -> x0, waiting for transfers between devices: 23.2 us -> none  [the longest x1 18.1 us: with_halo(): after = lax.ppermute(leading, axis, down)]
  transfers between devices with their start and end apart: 5 -> 0, of which waited for: 4 -> 0; matrix products, arithmetic and copies ran while one was open for 9% -> 0% of each run, Pallas kernels for 0% -> 0%
where the time goes in v1:
time: 210 us
  Pallas kernels  182 us (87%)
  local copies, waits for them, and re-layouts  19.7 us (9%)
  other arithmetic  7.44 us (4%)
    pallas_call x1, Pallas kernels, local(): pl.pallas_call(functools.partial(body, nf, nz, rows_a, rows_b), out_shape...  182 us
    unnamed x18, local copies, waits for them, and re-layouts  11.5 us

profile of v1, /device:TPU:0, one launch (start us, length us, event | category | flops | bytes accessed | tf_op | source)
XLA Modules:
  0.0 209.8 jit_solution(14642650490467104930)
XLA Ops:
  0.6 1.3 copy.36.grp
  2.0 0.7 constant_dynamic-update-slice_fusion.8
  2.7 0.7 constant_dynamic-update-slice_fusion.7
  3.4 0.7 constant_dynamic-update-slice_fusion.6
  4.0 0.7 constant_dynamic-update-slice_fusion.5
  4.7 0.7 constant_dynamic-update-slice_fusion.4
  5.4 0.7 constant_dynamic-update-slice_fusion.3
  6.1 0.7 constant_dynamic-update-slice_fusion.2
  6.8 0.7 constant_dynamic-update-slice_fusion.1
  7.5 0.7 constant_dynamic-update-slice_fusion
  8.2 0.6 reshape.77.vecs
  8.8 182.0 %shard_map.288 = (bf16[4,392,384]{2,1,0:T(8,128)(2,1)}, f32[4,4,384]{2,1,0:T(4,128)}, bf16[4,392,384]{2,1,0:T(8,128)(2,1)}, bf16[3584,384]{1,0:T(8,128)(2,1)}, bf16[1536,384]{1,0:T(8,128)(2,1)}) custom-call(bf16[4,392,384]{2,1,0:T(8,128)(2,1)} %tok.1, bf16[4,392,384]{2,1,0:T(8,128)(2,1)} %og.1, s32[4,2,392]{2,1,0:T(2,128)} %masks.1, s32[4,2]{1,0:T(4,128)} %copy.36.grp, ...), custom_call_target="tpu_custom_call" | custom-call | tf_op jit(solution)/shard_map/pallas_call | solution.py:756
  190.8 0.0 copy-start.2
  190.8 0.7 slice_convert_fusion.2
  191.5 0.6 reshape.84
  192.1 1.5 convert_reduce_fusion
  193.6 2.2 %slice.39 = bf16[1152,384]{1,0:T(8,128)(2,1)} slice(bf16[1536,384]{1,0:T(8,128)(2,1)} %get-tuple-element.24), slice={[0:1152], [0:384]} | slice | bytes 1769472 | tf_op jit(solution)/shard_map/slice | solution.py:841
  195.8 0.0 copy-done.2
  195.8 0.6 reshape.78
  196.4 1.8 slice_convert_fusion.1
  198.2 3.3 %slice_convert_fusion = (f32[1536,384]{1,0:T(8,128)}, bf16[1536,384]{1,0:T(8,128)(2,1)S(1)}) fusion(bf16[3584,384]{1,0:T(8,128)(2,1)} %get-tuple-element.25), kind=kLoop, calls=%fused_computation.1 | loop fusion | flops 589824 | bytes 5898240 | tf_op jit(solution)/shard_map/convert_element_type | solution.py:848
  201.5 1.8 copy.37
  203.3 1.9 copy.39
  205.2 0.2 convert_bitcast_fusion
  205.3 0.0 copy-start.1
  205.3 1.7 copy.40
  207.0 0.0 copy-done.1
  207.0 0.0 copy-start
  207.0 1.0 copy.52
  208.1 0.7 copy-done
  208.8 1.0 copy.53
  (1 shorter events, 0.0 us)
Async XLA Ops:
  190.8 5.0 %copy-start.2 = (f32[4,4,384]{2,1,0:T(4,128)S(1)}, f32[4,4,384]{2,1,0:T(4,128)}, u32[]{:S(2)}) copy-start(f32[4,4,384]{2,1,0:T(4,128)} %get-tuple-element.22) | copy-start | bytes 73732
  205.3 1.7 copy-start.1
  207.0 1.7 copy-start

commit v2 on v1

v2 whole, which is shorter than its diff:
```python
import functools

import jax
import jax.numpy as jnp
from jax import lax
from jax.experimental import pallas as pl
from jax.experimental.pallas import tpu as pltpu
from jax.sharding import PartitionSpec as P

HEADS = 6
NF = 8
HW = 196
GROUPS = 2
EPSILON = 1e-06
NEGATIVE = -1e30
MESH = pl.DeviceIdType.MESH
f32 = jnp.float32
bf16 = jnp.bfloat16

D = 384
FF = 1536
KR = 208
QL = 256
QB, VB, PB, UB, DB, G1, S1, G2, S2 = 0, 1, 2, 3, 7, 8, 9, 10, 11
G_UP, G_PROJ, G_QKV = FF, 2 * FF, 2 * FF + D
G_ROWS = G_QKV + 3 * D
CHUNKS = ((0, FF, False), (G_UP, FF, False), (G_PROJ, D, True))
CHUNKS += tuple((G_QKV + k * D, D, True) for k in range(3))
V_UB, V_PB, V_DB, V_G2, V_S2, V_QB, V_VB, V_G1, V_S1 = 0, 4, 5, 6, 7, 8, 9, 10, 11


def dot(a, b):
    return lax.dot_general(a, b, (((1,), (0,)), ((), ())), preferred_element_type=f32)


def dot_t(a, b):
    return lax.dot_general(a, b, (((1,), (1,)), ((), ())), preferred_element_type=f32)


def iota(shape, dim):
    return lax.broadcasted_iota(jnp.int32, shape, dim)


def low(v):
    return v.astype(bf16)


def wide(v):
    return jnp.concatenate([v, v], axis=1)


def fold(v):
    return v[:, 0:128] + v[:, 128:256]


def eye(n):
    return low(jnp.where(iota((n, n), 0) == iota((n, n), 1), 1.0, 0.0))


def ds(start, size, step):
    return pl.ds(pl.multiple_of(start, step), size)


def both(a, b):
    return b if a is None else a if b is None else jnp.logical_and(a, b)


def when(condition, action):
    if condition is None:
        action()
    else:
        pl.when(condition)(action)


def share(rows, n):
    return next(p for p in range(16, rows + 1, 16) if rows % p == 0 and p * n >= rows)


def spans(nf, nz):
    out, start = [], 0
    for _, rows, z_first in CHUNKS:
        n2, n3 = (nz, nf) if z_first else (nf, nz)
        part = share(rows // 2, n2)
        piece = part if z_first else share(part, n3)
        out.append((start, part, start + (n2 - 1) * part, piece))
        start += (n2 - 1) * part + (n3 - 1) * piece
    return out, start


def together(steps):
    steps = list(steps)
    while steps:
        steps = [s for s in steps if next(s, steps) is not steps]


class Reduce:
    def __init__(self, chunk, refs, sems, me, nf, nz):
        self.off, rows, self.z_first = CHUNKS[chunk]
        self.g, self.sb, self.ag, self.land = refs
        self.send, self.recv = sems[0].at[chunk], sems[1].at[chunk]
        self.f, clip = me
        self.core, self.z = lax.rem(clip, 2), lax.div(clip, 2)
        self.half = rows // 2
        self.land2, self.part, self.land3, self.piece = spans(nf, nz)[0][chunk]
        self.size = (nz, nf) if self.z_first else (nf, nz)
        n3 = self.size[1]
        self.own = (self.half // self.part, n3 if self.z_first else self.part // self.piece)
        self.pos = (self.z, self.f) if self.z_first else (self.f, self.z)
        self.base = self.off + self.core * self.half
        self.qbase = self.base + self.pos[0] * self.part
        self.pbase = self.qbase if self.z_first else self.qbase + self.pos[1] * self.piece

    def at(self, start, size, ref=None):
        return (self.ag if ref is None else ref).at[ds(start, size, 16), :]

    def landing(self, level, k):
        start, rows = ((self.land2, self.part), (self.land3, self.piece))[level]
        return self.land.at[pl.ds(start + k * rows, rows), :]

    def owns(self, level, pos=None):
        if self.own[level] == self.size[level]:
            return None
        return (self.pos[level] if pos is None else pos) < self.own[level]

    def peer(self, level, k):
        t = lax.rem(self.pos[level] + k, self.size[level])
        along_z = self.z_first == (level == 0)
        dev = (self.f, t * 2 + self.core) if along_z else (t, self.z * 2 + self.core)
        return t, dev

    def copies(self, stage):
        n2, n3 = self.size
        out = []
        if stage == 1:
            o = self.at(self.off + (1 - self.core) * self.half, self.half, self.sb)
            out = [(o, o, (self.f, self.z * 2 + 1 - self.core), 0, None, None)]
        if stage in (2, 5):
            for k in range(1, n2):
                t, dev = self.peer(0, k)
                if stage == 2:
                    src = self.at(self.base + t * self.part, self.part, self.sb)
                    dst = self.landing(0, k - 1)
                    out.append((src, dst, dev, k, self.owns(0, t), self.owns(0)))
                else:
                    s, _ = self.peer(0, n2 - k)
                    src = self.at(self.qbase, self.part)
                    sem = n2 + 2 * n3 + k - 3
                    out.append((src, src, dev, sem, self.owns(0), self.owns(0, s)))
        if stage == 3 or (stage == 4 and not self.z_first):
            for k in range(1, n3):
                t, dev = self.peer(1, k)
                if stage == 3:
                    first = self.qbase if self.z_first else self.qbase + t * self.piece
                    src = self.at(first, self.piece, self.sb)
                    sent, comes = self.owns(1, t), self.owns(1)
                    out.append((src, self.landing(1, k - 1), dev, n2 + k - 1, sent, comes))
                else:
                    s, _ = self.peer(1, n3 - k)
                    src = self.at(self.pbase, self.piece)
                    out.append((src, src, dev, n2 + n3 + k - 2, self.owns(1), self.owns(1, s)))
            part = self.owns(0)
            if part is not None:
                out = [(*c[:4], both(part, c[4]), both(part, c[5])) for c in out]
        if stage == 6:
            s = self.at(self.base, self.half)
            dev = (self.f, self.z * 2 + 1 - self.core)
            out = [(s, s, dev, 2 * n2 + 2 * n3 - 3, None, None)]
        return [
            (
                pltpu.make_async_remote_copy(
                    src_ref=s,
                    dst_ref=d,
                    send_sem=self.send.at[i],
                    recv_sem=self.recv.at[i],
                    device_id=dev,
                    device_id_type=MESH,
                ),
                sent,
                comes,
            )
            for s, d, dev, i, sent, comes in out
        ]

    def start(self, stage):
        for c, sent, _ in self.copies(stage):
            when(sent, c.start)

    def wait(self, stage):
        for c, sent, comes in self.copies(stage):
            when(comes, c.wait_recv)
            when(sent, c.wait_send)

    def step(self, stage):
        if stage > 1:
            self.wait(stage - 1)
        g, sb, ag = self.g, self.sb, self.ag
        n2, n3 = self.size
        if stage == 1:
            rows = ds(self.off + (1 - self.core) * self.half, self.half, 16)
            sb[rows, :] = low(g[rows, :])
        if stage == 2:
            rows = ds(self.base, self.half, 16)
            total = g[rows, :] + sb[rows, :].astype(f32)
            g[rows, :] = total
            sb[rows, :] = low(total)
        if stage == 3:

            def sum_part():
                rows = ds(self.qbase, self.part, 16)
                total = g[rows, :]
                for k in range(n2 - 1):
                    total += self.landing(0, k)[...].astype(f32)
                g[rows, :] = total
                sb[rows, :] = low(total)

            when(self.owns(0), sum_part)
        if stage == 4:

            def sum_piece():
                rows = ds(self.pbase, self.piece, 16)
                total = g[rows, :]
                for k in range(n3 - 1):
                    total += self.landing(1, k)[...].astype(f32)
                ag[rows, :] = low(total)

            when(both(self.owns(0), self.owns(1)), sum_piece)
        if stage < 7:
            self.start(stage)

    @staticmethod
    def count(nf, nz):
        return 2 * nf + 2 * nz - 2


def body(
    nf,
    nz,
    tok,
    og,
    masks,
    grp,
    wqkv,
    wp,
    wu,
    wd,
    vqb,
    vvb,
    vpb,
    vub,
    vdb,
    vg1,
    vs1,
    vg2,
    vs2,
    bout,
    stats,
    gtok,
    out_g,
    out_v,
    wqvT,
    wpT,
    wuT,
    wdT,
    cb,
    TI,
    OS,
    xs,
    ys,
    mw,
    XT,
    n1T,
    NR,
    QT,
    KT,
    VT,
    Kr,
    Vr,
    ctxT,
    n2T,
    AD,
    gattT,
    dyR,
    dOT,
    dyT,
    FX,
    FY,
    SS,
    PG,
    SG,
    ST,
    dmid,
    DQ,
    acc,
    SP,
    SPr,
    G,
    SB,
    AG,
    RL,
    VS,
    V1,
    V2,
    nr_send,
    nr_recv,
    do_send,
    do_recv,
    st_send,
    st_recv,
    sp_send,
    sp_recv,
    red_send,
    red_recv,
    vec_send,
    vec_recv,
    out_sem,
    in_sem,
    row_sem,
):
    clips = tok.shape[0]
    rows = tok.shape[1]
    me_f = lax.axis_index("frame")
    me_c = lax.axis_index("clip")
    core, zi = lax.rem(me_c, 2), lax.div(me_c, 2)
    first, last = me_f == 0, me_f == nf - 1

    def fetch(ref, k, c):
        return pltpu.make_async_copy(ref.at[c], TI.at[c], in_sem.at[k, c])

    def put(n, ref, c):
        slot = lax.rem(n, 2)
        cp = pltpu.make_async_copy(OS.at[slot], ref.at[c], row_sem.at[slot])
        pl.when(n >= 2)(cp.wait)
        OS[slot] = low(ys[0:rows, :])
        cp.start()

    for c in range(clips):
        fetch(tok, 0, c).start()

    NR[...] = jnp.zeros(NR.shape, bf16)
    for c in range(clips):
        for s in (0, 3):
            dOT[c * 4 + s] = jnp.zeros(dOT.shape[1:], bf16)
            ST[c * 4 + s] = jnp.where(iota((3, 8, QL), 1) < 2, 1e30, 0.0)

    barrier = pltpu.get_barrier_semaphore()
    near = [
        (lax.rem(me_f + k, nf), zi * 2 + lax.rem(core + m, 2))
        for k in range(nf)
        for m in range(2)
        if k or m
    ]
    far = [(me_f, lax.rem(zi + k, nz) * 2 + core) for k in range(1, nz)]
    peers = near + far
    for peer in peers:
        pl.semaphore_signal(barrier, inc=1, device_id=peer, device_id_type=MESH)

    def halo(src, dst, send, recv, to_right):
        return pltpu.make_async_remote_copy(
            src_ref=src,
            dst_ref=dst,
            send_sem=send,
            recv_sem=recv,
            device_id=((me_f + 1) if to_right else (me_f - 1), me_c),
            device_id_type=MESH,
        )

    def nr_copy(c, right):
        i, o, k = (2, 0, 0) if right else (1, 3, 1)
        return halo(
            NR.at[c * 4 + i, pl.ds(0, KR)],
            NR.at[c * 4 + o, pl.ds(0, KR)],
            nr_send.at[c, k],
            nr_recv.at[c, k],
            right,
        )

    def do_copies(c, right):
        i, o, k = (2, 0, 0) if right else (1, 3, 1)
        return (
            halo(
                dOT.at[c * 4 + i], dOT.at[c * 4 + o], do_send.at[c, k], do_recv.at[c, k], right
            ),
            halo(ST.at[c * 4 + i], ST.at[c * 4 + o], st_send.at[c, k], st_recv.at[c, k], right),
        )

    def each_side(start, make):
        for right, here, there in ((True, last, first), (False, first, last)):

            @pl.when(jnp.logical_not(here))
            def _():
                for cp in make(right):
                    if start:
                        cp.start()
                    else:
                        cp.wait_send()

            if not start:

                @pl.when(jnp.logical_not(there))
                def _():
                    for cp in make(right):
                        cp.wait_recv()

    xs[...] = jnp.zeros(xs.shape, f32)
    mw[...] = jnp.zeros(mw.shape, f32)
    one_d = eye(D)
    one_q = eye(QL)

    def column(i):
        return wide(cb[i])

    def as_row(ref, k):
        return ref[k * D : (k + 1) * D].reshape(1, D)

    table = [(vqb, 0), (vvb, 0), (vpb, 0)] + [(vub, k) for k in range(4)]
    table += [(v, 0) for v in (vdb, vg1, vs1, vg2, vs2)]
    for i, (ref, k) in enumerate(table):
        cb[i] = jnp.transpose(jnp.broadcast_to(as_row(ref, k), (128, D)))
    n1T[...] = jnp.ones(n1T.shape, bf16)
    n2T[...] = jnp.ones(n2T.shape, bf16)
    ctxT[...] = jnp.ones(ctxT.shape, bf16)
    def frame_rows(f):
        v = xs[pl.ds(HW * f, KR), :]
        tail = jnp.where(iota((16, D), 0) < HW - (KR - 16), v[KR - 16 :], 0.0)
        return low(jnp.concatenate([v[: KR - 16], tail, jnp.zeros((QL - KR, D), f32)], axis=0))

    def norm_one(c):
        xs[0:rows, :] = TI[c].astype(f32)
        for f in range(2):
            xT = dot_t(one_d, frame_rows(f))
            XT[c * 2 + f] = low(xT)
            cent = xT - jnp.sum(xT, axis=0, keepdims=True) * (1.0 / D)
            var = jnp.sum(cent * cent, axis=0, keepdims=True) * (1.0 / D)
            nT = low(cent * lax.rsqrt(var + EPSILON) * column(G1) + column(S1))
            n1T[0:D, ds((c * 2 + f) * QL, QL, QL)] = nT
            NR[c * 4 + f + 1, 0:KR, :] = low(dot_t(one_q[0:KR], nT))

    def turn(j):
        if j < 2:
            col = (0, 2 * D)[j]
            wqvT[j * D : (j + 1) * D, :] = low(dot_t(one_d, wqkv[:, col : col + D]))
        if j == 2:
            wpT[...] = low(dot_t(one_d, wp[...]))
        wuT[j * D : (j + 1) * D, :] = low(dot_t(one_d, wu[:, j * D : (j + 1) * D]))
        wdT[:, j * D : (j + 1) * D] = low(dot_t(one_d, wd[j * D : (j + 1) * D, :]))

    fetch(tok, 0, 0).wait()
    norm_one(0)
    pl.semaphore_wait(barrier, len(peers))
    each_side(True, lambda right: (nr_copy(0, right),))
    for c in range(1, clips):
        fetch(tok, 0, c).wait()
    for n in range(1, max(clips, 5)):
        if n < clips:
            norm_one(n)
        if n < 5:
            turn(n - 1)
    for c in range(clips):
        fetch(og, 1, c).start()

    for r in (G, VS, acc):
        r[...] = jnp.zeros(r.shape, f32)
    KT[...] = jnp.zeros(KT.shape, bf16)
    SG[...] = jnp.zeros(SG.shape, bf16)

    before_bias = jnp.where(first, NEGATIVE, 0.0).astype(f32)
    after_bias = jnp.where(last, NEGATIVE, 0.0).astype(f32)
    z64 = jnp.zeros((64, QL), bf16)
    zpad = jnp.zeros((QL - KR, QL), bf16)

    def split_heads(v):
        return (
            jnp.concatenate([v[0:64], z64], axis=0),
            jnp.concatenate([z64, v[64:128]], axis=0),
        )

    def project(c, s):
        i = c * 4 + s
        own = s in (1, 2)
        t = dot_t(wqvT[...] if own else wqvT[D:, :], NR[i])
        if own:
            put_queries(i, t[0:D])
        vT = low(t[-D:] + column(VB))
        k = low(dot(NR[i, 0:KR], wqkv[:, D : 2 * D]))
        for p in range(3):
            sl = slice(p * 128, (p + 1) * 128)
            VT[s, p] = vT[sl]
            Kr[i, p] = k[:, sl]

    def put_queries(i, t):
        qT = low(low(t + column(QB)) * 0.125)
        for p in range(3):
            QT[i, p] = qT[p * 128 : (p + 1) * 128]

    def project_back(c):
        for s in range(4):
            i = c * 4 + s
            v = low(dot(NR[i, 0:KR], wqkv[:, 2 * D :]) + as_row(vvb, 0))
            for p in range(3):
                Vr[i, p] = v[:, p * 128 : (p + 1) * 128]
            if s in (0, 3):
                put_queries(i, dot_t(wqvT[0:D, :], NR[i]))

    def ss(k):
        return SS.at[k]

    def one_head(v, hh):
        return split_heads(v)[hh]

    def mask_tail(v, fill):
        tail = jnp.where(iota((16, QL), 0) < HW - (KR - 16), v[KR - 16 :], fill)
        return jnp.concatenate([v[: KR - 16], tail], axis=0)

    def forward(c):
        units = [(f, p, hh) for p in range(3) for f in range(2) for hh in range(2)]
        tops, totals, held = {}, {}, {}

        def scores(u, par):
            f, p, hh = u
            q = one_head(QT[c * 4 + f + 1, p], hh)
            tops_j = []
            for j in range(3):
                s = mask_tail(dot(Kr[c * 4 + f + j, p], q), NEGATIVE)
                if f + j == 0:
                    s = s + before_bias
                if f + j == 3:
                    s = s + after_bias
                ss(par * 4 + j)[...] = s
                tops_j.append(jnp.max(s, axis=0, keepdims=True))
                yield
            tops[u] = functools.reduce(jnp.maximum, tops_j)

        def soft(u, par):
            total = jnp.zeros((1, QL), f32)
            for j in range(3):
                e = jnp.exp(ss(par * 4 + j)[...] - tops[u])
                total += jnp.sum(e, axis=0, keepdims=True)
                SG[par, 0:KR, j * QL : (j + 1) * QL] = low(e)
                yield
            totals[u] = total
            f, p, hh = u
            ST[c * 4 + f + 1, p, hh : hh + 1, :] = tops[u] + jnp.log(total)

        def context(u, par):
            f, p, hh = u
            ctx = jnp.zeros((64, QL), f32)
            for j in range(3):
                e = SG[par, :, j * QL : (j + 1) * QL]
                ctx += dot(VT[f + j, p, hh * 64 : hh * 64 + 64, :], e)
                yield
            at = p * 128 + hh * 64
            ctxT[at : at + 64, f * QL : (f + 1) * QL] = low(ctx * (1.0 / totals[u]))

        for n in range(len(units) + 2):
            steps = []
            if n < len(units):
                steps.append(scores(units[n], n % 2))
            if 1 <= n <= len(units):
                steps.append(soft(units[n - 1], (n - 1) % 2))
            if n >= 2:
                steps.append(context(units[n - 2], n % 2))
            together(steps)

    def gelu_parts(v):
        t = 1.0 / (1.0 + (0.3275911 * 0.7071067811865476) * jnp.abs(v))
        e = jnp.exp2(v * v * (-0.5 * 1.4426950408889634))
        poly = 0.5 * 1.061405429
        poly = poly * t + 0.5 * -1.453152027
        poly = poly * t + 0.5 * 1.421413741
        poly = poly * t + 0.5 * -0.284496736
        poly = poly * t + 0.5 * 0.254829592
        h = poly * t * e
        phi = jnp.where(v >= 0, 1.0 - h, h)
        return phi, v * (e * 0.3989422804014327)

    def feed_forward(c):
        lanes = [slice(f * QL, (f + 1) * QL) for f in range(2)]
        keep = [None, None]

        def enter(f):
            xT = XT[c * 2 + f].astype(f32)
            mid = xT + (dot(wpT[...], ctxT[0:D, lanes[f]]) + column(PB))
            cent = mid - jnp.sum(mid, axis=0, keepdims=True) * (1.0 / D)
            var = jnp.sum(cent * cent, axis=0, keepdims=True) * (1.0 / D)
            r = lax.rsqrt(var + EPSILON)
            xh = cent * r
            n2T[0:D, lanes[f]] = low(xh * column(G2) + column(S2))
            dmid[c * 2 + f] = mid
            FY[f] = xh
            dy = frame_rows(f)
            dyR[lanes[f], :] = dy
            dyT[f] = low(dot_t(one_d, dy))
            keep[f] = r

        def act_at(k, f, j):
            return slice(k * 24 + f * 12 + 3 * j, k * 24 + f * 12 + 3 * j + 3)

        def products(u, par):
            f, j = u
            for k in range(2):
                rows_k = slice(k * 192, (k + 1) * 192)
                sl = slice(j * D + k * 192, j * D + (k + 1) * 192)
                bias = wide(cb[UB + j, rows_k, :])
                FX[2 * par, rows_k, :] = dot(wuT[sl, :], n2T[0:D, lanes[f]]) + bias
                yield
                FX[2 * par + 1, rows_k, :] = dot(wd[sl, :], dyT[f])
                yield

        def nonlinear(u, par):
            f, j = u
            for k in range(3):
                sl = slice(k * 128, (k + 1) * 128)
                pre = FX[2 * par, sl, :]
                phi, slope = gelu_parts(pre)
                AD[f * 12 + 3 * j + k] = low(pre * phi)
                AD[24 + f * 12 + 3 * j + k] = low(FX[2 * par + 1, sl, :] * (phi + slope))
                yield

        def leave(f):
            outT = dot(wdT[...], AD[f * 12 : f * 12 + 12].reshape(FF, QL))
            outT += dmid[c * 2 + f] + column(DB)
            dn = dot(wu[...], AD[24 + f * 12 : 36 + f * 12].reshape(FF, QL))
            return outT, dn

        def finish_frame(f, outT, dn):
            outl = low(outT)
            ys[pl.ds(HW * f, KR), :] = dot_t(one_q[0:KR], outl)
            sq = outT * outT
            out2 = low(outT - outl.astype(f32))
            sql = low(sq)
            sq2 = low(sq - sql.astype(f32))
            m = mw[...]
            if f == 1:
                m = pltpu.roll(m, 2 * QL - HW, 1)
            m = jnp.where(iota((8, QL), 1) < HW, m[:, 0:QL], 0.0)
            w = []
            for g in range(GROUPS):
                w.append(
                    sum(
                        m[v : v + 1, :] * jnp.where(grp[v, c] == g, 1.0, 0.0).astype(f32)
                        for v in range(2)
                    )
                )
            row = iota((16, QL), 0)

            def place(k):
                return jnp.where(row == k, w[0], jnp.where(row == k + 1, w[1], 0.0))

            w1, w2 = low(place(0)), low(place(2))
            cnt = jnp.sum(place(4), axis=1, keepdims=True)
            sums = dot_t(w1, outl) + dot_t(w1, out2) + dot_t(w2, sql) + dot_t(w2, sq2) + cnt
            if f == 0:
                SP[c] = sums[0:8]
            else:
                SP[c] = SP[c] + sums[0:8]
            xh = FY[f]
            acc[0] += fold(dn * xh)
            acc[1] += fold(dn)
            gg = dn * column(G2)
            m1 = jnp.sum(gg, axis=0, keepdims=True) * (1.0 / D)
            m2 = jnp.sum(gg * xh, axis=0, keepdims=True) * (1.0 / D)
            gm = dyT[f].astype(f32) + keep[f] * (gg - m1 - xh * m2)
            dmid[c * 2 + f] = gm
            ga = low(gm)
            gattT[:, lanes[f]] = ga
            gc = low(dot(wp[...], ga))
            i = c * 4 + f + 1
            prod = gc.astype(f32) * ctxT[0:D, lanes[f]].astype(f32)
            for h in range(HEADS):
                ST[i, h // 2, 2 + h % 2 : 3 + h % 2, :] = jnp.sum(
                    prod[h * 64 : h * 64 + 64], axis=0, keepdims=True
                )
            for p in range(3):
                dOT[i, p] = gc[p * 128 : (p + 1) * 128]

        def both(k, j):
            return jnp.concatenate([AD[act_at(k, f, j)].reshape(D, QL) for f in range(2)], axis=1)

        units = [(f, j) for f in range(2) for j in range(4)]
        left = {}
        enter(0)
        for n in range(len(units) + 1):
            steps = []
            if n < len(units):
                steps.append(products(units[n], n % 2))
            if n >= 1:
                steps.append(nonlinear(units[n - 1], (n - 1) % 2))
            if n == 1:
                enter(1)
            together(steps)
            if n == 5:
                left[0] = leave(0)
            if n == 6:
                finish_frame(0, *left[0])
        left[1] = leave(1)
        for j in range(4):
            G[j * D : (j + 1) * D, :] += dot(both(0, j), dyR[...])
        finish_frame(1, *left[1])
        for j in range(4):
            g = dot_t(n2T[...], both(1, j))
            G[G_UP + j * D : G_UP + (j + 1) * D, :] += g[0:D]
            VS[V_UB + j : V_UB + j + 1, :] += g[D : D + 1]
        g = dot_t(ctxT[...], gattT[...])
        G[G_PROJ:G_QKV, :] += g[0:D]
        VS[V_PB : V_PB + 1, :] += g[D : D + 1]
        VS[V_DB : V_DB + 1, :] += dot(n2T[D : D + 16, :], dyR[...])[0:1]

    def front(c, _):
        project(c, 1)
        project(c, 2)
        each_side(False, lambda right: (nr_copy(c, right),))

        @pl.when(c == 0)
        def _():
            each_side(True, lambda right: (nr_copy(1, right),))

        project(c, 0)
        project(c, 3)

        forward(c)

        @pl.when(c == 0)
        def _():
            for n in range(2, clips):
                each_side(True, lambda right: (nr_copy(n, right),))

        fetch(og, 1, c).wait()
        xs[0:rows, :] = TI[c].astype(f32)
        mw[0:2, 0:rows] = masks[c].astype(f32)
        feed_forward(c)
        each_side(True, lambda right: do_copies(c, right))
        put(c, bout, c)
        return 0

    lax.fori_loop(0, clips, front, 0)

    def gather_rows(row, k):
        VS[row : row + 1, :] = jnp.sum(jnp.transpose(acc[k]), axis=0, keepdims=True)

    gather_rows(V_G2, 0)
    gather_rows(V_S2, 1)

    me = (me_f, me_c)
    refs, red_sems = (G, SB, AG, RL), (red_send, red_recv)
    red = [Reduce(k, refs, red_sems, me, nf, nz) for k in range(len(CHUNKS))]
    for k in range(3):
        red[k].step(1)

    def sp_copies():
        return [
            pltpu.make_async_remote_copy(
                src_ref=SP,
                dst_ref=SPr.at[k - 1],
                send_sem=sp_send.at[k - 1],
                recv_sem=sp_recv.at[k - 1],
                device_id=(lax.rem(me_f + k, nf), me_c),
                device_id_type=MESH,
            )
            for k in range(1, nf)
        ]

    for cp in sp_copies():
        cp.start()

    has_before = jnp.where(first, 0.0, 1.0).astype(f32)
    has_after = jnp.where(last, 0.0, 1.0).astype(f32)

    def back_pair(c, p):
        blocks = [(0, 1), (1, 1), (2, 1), (1, 0), (1, 2), (2, 2), (3, 2), (2, 3)]
        units = [(q, g, hh) for q, g in blocks for hh in range(2)]

        def lanes_of(q, g, hh):
            k = ((q - g + 1) if g in (1, 2) else 3) * 2 + hh
            return (0 if g < 2 else 1), slice(k * QL, (k + 1) * QL)

        def products(u, par):
            q, g, hh = u
            ss(2 * par)[...] = dot(Kr[c * 4 + g, p], one_head(QT[c * 4 + q, p], hh))
            yield
            ss(2 * par + 1)[...] = dot(Vr[c * 4 + g, p], one_head(dOT[c * 4 + q, p], hh))
            yield

        def gradient(u, par):
            q, g, hh = u
            i = c * 4 + q
            side, at = lanes_of(q, g, hh)
            keep = {0: has_before, 3: has_after}.get(g)
            for lo, hi in ((0, 112), (112, KR)):
                pr = jnp.exp(ss(2 * par)[lo:hi, :] - ST[i, p, hh : hh + 1, :])
                if keep is not None:
                    pr = pr * keep
                if hi == KR:
                    tail = jnp.where(iota((16, QL), 0) < HW - (KR - 16), pr[KR - 16 - lo :], 0.0)
                    pr = jnp.concatenate([pr[: KR - 16 - lo], tail], axis=0)
                if g in (1, 2):
                    PG[side, lo:hi, at] = low(pr)
                dp = ss(2 * par + 1)[lo:hi, :] - ST[i, p, 2 + hh : 3 + hh, :]
                SG[side, lo:hi, at] = low(pr * dp)
                yield

        def keys_done(g):
            side, f = g - 1, g - 1
            qs = [c * 4 + g - 1 + k for k in range(3)]
            doms = jnp.concatenate([one_head(dOT[i, p], hh) for i in qs for hh in range(2)], axis=1)
            qms = jnp.concatenate([one_head(QT[i, p], hh) for i in qs for hh in range(2)], axis=1)
            gv = dot_t(PG[side], doms)
            gk = dot_t(SG[side, 0:KR, 0 : 6 * QL], qms)
            kv = jnp.concatenate([low(jnp.concatenate([gk, gv], axis=1)), zpad], axis=0)
            AD[pl.ds(2 * (p * 2 * clips + c * 2 + f), 2)] = kv.reshape(2, 128, QL)

        def queries_done(q):
            out = []
            for hh in range(2):
                total = jnp.zeros((64, QL), f32)
                for g in (q - 1, q, q + 1):
                    side, at = lanes_of(q, g, hh)
                    total += dot(KT[g, hh * 64 : hh * 64 + 64, :], SG[side, :, at])
                out.append(total)
            DQ[p, :, ds((c * 2 + q - 1) * QL, QL, QL)] = low(
                jnp.concatenate(out, axis=0) * 0.125
            )

        for n in range(len(units) + 1):
            steps = []
            if n < len(units):
                steps.append(products(units[n], n % 2))
            if n >= 1:
                steps.append(gradient(units[n - 1], (n - 1) % 2))
            together(steps)
            if n == 7:
                keys_done(1)
            if n == 11:
                queries_done(1)
            if n == 15:
                keys_done(2)
        queries_done(2)

    plan = {
        0: ((0, 2),),
        1: ((1, 2), (2, 2)),
        3: ((3, 1),),
        4: ((0, 3), (3, 2)),
        5: ((2, 3),),
        6: ((0, 4),),
        7: ((4, 1), (1, 3)),
        8: ((0, 5), (3, 3), (4, 2), (2, 4)),
        9: ((1, 4),),
        11: ((5, 1), (1, 5), (3, 4), (2, 5)),
        12: ((5, 2), (4, 3)),
        13: ((3, 5), (0, 6)),
        14: ((4, 4), (2, 6)),
        15: ((5, 3), (3, 6), (1, 6)),
    }
    after_vectors = (((4, 5), (5, 4), (5, 5)), ((4, 6),))

    def advance(it):
        for when_it, steps in plan.items():

            @pl.when(it == when_it)
            def _():
                for k, stage in steps:
                    red[k].step(stage)

    def qkv_grad(p):
        kv = AD[pl.ds(p * 4 * clips, 4 * clips)].reshape(2 * clips * QL, QL)
        g = jnp.concatenate([dot_t(n1T[...], DQ[p]), dot(n1T[...], kv)], axis=1)
        G[ds(G_QKV + p * D, D, D), :] = g[0:D]
        at = pl.ds(pl.multiple_of(p * 128, 128), 128)
        VS[V_QB : V_QB + 1, at] = g[D : D + 1, 0:128]
        VS[V_VB : V_VB + 1, at] = g[D : D + 1, 2 * 128 :]

    def back(it, _):
        c, p = lax.rem(it, clips), lax.div(it, clips)

        @pl.when(p == 0)
        def _():
            project_back(c)
            each_side(False, lambda right: do_copies(c, right))

        for g in range(4):
            KT[g, :, 0:KR] = low(dot_t(one_q[0:128, 0:128], Kr[c * 4 + g, p]))
        back_pair(c, p)

        @pl.when(c == clips - 1)
        def _():
            qkv_grad(p)

        advance(it)
        return 0

    lax.fori_loop(0, 3 * clips, back, 0)

    def last_norm(c, _):
        for f in range(2):
            b = c * 2 + f
            lanes = ds(b * QL, QL, QL)
            dq = jnp.concatenate([DQ[p, :, lanes] for p in range(3)], axis=0)
            kv = [AD[pl.ds(2 * (p * 2 * clips + b), 2)].reshape(QL, QL) for p in range(3)]
            dk = jnp.concatenate([v[:, 0:128] for v in kv], axis=1)
            dv = jnp.concatenate([v[:, 128:256] for v in kv], axis=1)
            dn = dot(wqkv[:, 0:D], dq) + dot_t(wqkv[:, D : 2 * D], dk)
            dn += dot_t(wqkv[:, 2 * D :], dv)
            xT = XT[b].astype(f32)
            cent = xT - jnp.sum(xT, axis=0, keepdims=True) * (1.0 / D)
            var = jnp.sum(cent * cent, axis=0, keepdims=True) * (1.0 / D)
            r = lax.rsqrt(var + EPSILON)
            xh = cent * r
            acc[2] += fold(dn * xh)
            acc[3] += fold(dn)
            gg = dn * column(G1)
            m1 = jnp.sum(gg, axis=0, keepdims=True) * (1.0 / D)
            m2 = jnp.sum(gg * xh, axis=0, keepdims=True) * (1.0 / D)
            gT = low(dmid[b] + r * (gg - m1 - xh * m2))
            ys[pl.ds(HW * f, KR), :] = dot_t(one_q[0:KR], gT)
        put(clips + c, gtok, c)
        advance(3 * clips + c)
        return 0

    lax.fori_loop(0, clips, last_norm, 0)
    gather_rows(V_G1, 2)
    gather_rows(V_S1, 3)

    def out_copy(k):
        off, n, _ = CHUNKS[k]
        rows = pl.ds(off, n)
        return pltpu.make_async_copy(AG.at[rows], out_g.at[rows], out_sem.at[k])

    def group_results():
        for cp in sp_copies():
            cp.wait()
        for c in range(clips):
            t = SP[c] + sum(SPr[k, c] for k in range(nf - 1))
            inv = 1.0 / jnp.maximum(t[4:6], 1.0)
            mean = t[0:2] * inv
            var = t[2:4] * inv - mean * mean
            stats[c, 0:1, :] = mean[0:1]
            stats[c, 1:2, :] = var[0:1]
            stats[c, 2:3, :] = mean[1:2]
            stats[c, 3:4, :] = var[1:2]

    groups = ((V1, near, 0), (V2, far, len(near)))
    for n, (dst, devs, at) in enumerate(groups):
        cps = [
            pltpu.make_async_remote_copy(
                src_ref=VS.at[pl.ds(16 * n, 16)],
                dst_ref=dst.at[k],
                send_sem=vec_send.at[at + k],
                recv_sem=vec_recv.at[at + k],
                device_id=dev,
                device_id_type=MESH,
            )
            for k, dev in enumerate(devs)
        ]
        for cp in cps:
            cp.start()
        for k, stage in after_vectors[n]:
            red[k].step(stage)
        if n == 0:
            group_results()
        for k in ((0, 3), (1, 2))[n]:
            red[k].step(7)
            out_copy(k).start()
        for cp in cps:
            cp.wait()
        total = VS[16 * n : 16 * n + 16, :]
        for k in range(len(devs)):
            total += dst[k]
        VS[16 * (n + 1) : 16 * (n + 2), :] = total
    copy_v = pltpu.make_async_copy(VS.at[pl.ds(32, 16)], out_v, out_sem.at[len(CHUNKS)])
    copy_v.start()

    red[5].step(6)
    for k in (4, 5):
        red[k].step(7)
        out_copy(k).start()
    for slot in range(2):
        pltpu.make_async_copy(OS.at[slot], gtok.at[0], row_sem.at[slot]).wait()
    for k in range(len(CHUNKS)):
        out_copy(k).wait()
    copy_v.wait()


def local(nf, nz, tokens, out_grad, view_masks, view_group, *params):
    w_qkv, query_bias, value_bias, w_proj, proj_bias, w_up, up_bias, w_down = params[:8]
    clips, rows, width = tokens.shape
    vmem = pl.BlockSpec(memory_space=pltpu.VMEM)
    hbm = pl.BlockSpec(memory_space=pl.ANY)
    sems = pltpu.SemaphoreType.DMA
    n_red = Reduce.count(nf, nz)
    _, landing = spans(nf, nz)
    bout, stats, gtok, out_g, out_v = pl.pallas_call(
        functools.partial(body, nf, nz),
        out_shape=(
            jax.ShapeDtypeStruct((clips, rows, D), bf16),
            jax.ShapeDtypeStruct((clips, 4, D), f32),
            jax.ShapeDtypeStruct((clips, rows, D), bf16),
            jax.ShapeDtypeStruct((G_ROWS, D), bf16),
            jax.ShapeDtypeStruct((16, D), f32),
        ),
        in_specs=[hbm, hbm, vmem, pl.BlockSpec(memory_space=pltpu.SMEM)] + [vmem] * 13,
        out_specs=(hbm, vmem, hbm, hbm, hbm),
        scratch_shapes=[
            pltpu.VMEM((2 * D, D), bf16),
            pltpu.VMEM((D, D), bf16),
            pltpu.VMEM((FF, D), bf16),
            pltpu.VMEM((D, FF), bf16),
            pltpu.VMEM((12, D, 128), f32),
            pltpu.VMEM((clips, rows, D), bf16),
            pltpu.VMEM((2, rows, D), bf16),
            pltpu.VMEM((408, D), f32),
            pltpu.VMEM((408, D), f32),
            pltpu.VMEM((8, 2 * QL), f32),
            pltpu.VMEM((clips * 2, D, QL), bf16),
            pltpu.VMEM((D + 16, clips * 2 * QL), bf16),
            pltpu.VMEM((clips * 4, QL, D), bf16),
            pltpu.VMEM((clips * 4, 3, 128, QL), bf16),
            pltpu.VMEM((4, 128, QL), bf16),
            pltpu.VMEM((4, 3, 128, QL), bf16),
            pltpu.VMEM((clips * 4, 3, KR, 128), bf16),
            pltpu.VMEM((clips * 4, 3, KR, 128), bf16),
            pltpu.VMEM((D + 16, 2 * QL), bf16),
            pltpu.VMEM((D + 16, 2 * QL), bf16),
            pltpu.VMEM((48, 128, QL), bf16),
            pltpu.VMEM((D, 2 * QL), bf16),
            pltpu.VMEM((2 * QL, D), bf16),
            pltpu.VMEM((clips * 4, 3, 128, QL), bf16),
            pltpu.VMEM((2, D, QL), bf16),
            pltpu.VMEM((4, D, QL), f32),
            pltpu.VMEM((2, D, QL), f32),
            pltpu.VMEM((8, KR, QL), f32),
            pltpu.VMEM((2, KR, 6 * QL), bf16),
            pltpu.VMEM((2, QL, 8 * QL), bf16),
            pltpu.VMEM((clips * 4, 3, 8, QL), f32),
            pltpu.VMEM((clips * 2, D, QL), f32),
            pltpu.VMEM((3, 128, clips * 2 * QL), bf16),
            pltpu.VMEM((4, D, 128), f32),
            pltpu.VMEM((clips, 8, D), f32),
            pltpu.VMEM((nf - 1, clips, 8, D), f32),
            pltpu.VMEM((G_ROWS, D), f32),
            pltpu.VMEM((G_ROWS, D), bf16),
            pltpu.VMEM((G_ROWS, D), bf16),
            pltpu.VMEM((landing, D), bf16),
            pltpu.VMEM((48, D), f32),
            pltpu.VMEM((2 * nf - 1, 16, D), f32),
            pltpu.VMEM((nz - 1, 16, D), f32),
            sems((clips, 2)),
            sems((clips, 2)),
            sems((clips, 2)),
            sems((clips, 2)),
            sems((clips, 2)),
            sems((clips, 2)),
            sems((nf - 1,)),
            sems((nf - 1,)),
            sems((len(CHUNKS), n_red)),
            sems((len(CHUNKS), n_red)),
            sems((2 * nf + nz - 2,)),
            sems((2 * nf + nz - 2,)),
            sems((len(CHUNKS) + 1,)),
            sems((2, clips)),
            sems((2,)),
        ],
        compiler_params=pltpu.CompilerParams(
            collective_id=0, has_side_effects=True, vmem_limit_bytes=64 * 1024 * 1024 - 65536
        ),
    )(
        tokens,
        out_grad,
        view_masks,
        view_group.T,
        w_qkv,
        w_proj,
        w_up,
        w_down,
        query_bias,
        value_bias,
        proj_bias,
        up_bias,
        *params[8:],
    )

    shape = jax.ShapeDtypeStruct
    outs = pl.pallas_call(
        finish,
        out_shape=(
            shape(bout.shape, bf16),
            shape(gtok.shape, bf16),
            shape((D, 3 * D), f32),
            shape((D, D), f32),
            shape((D, FF), f32),
            shape((FF, D), f32),
        )
        + (shape((D,), f32),) * 3
        + (shape((FF,), f32),)
        + (shape((D,), f32),) * 5
        + (shape((clips, GROUPS, 2, D), f32),),
        in_specs=[hbm] * 4 + [vmem],
        out_specs=(hbm,) * 6 + (vmem,) * 10,
        scratch_shapes=[
            pltpu.VMEM((G_ROWS, D), bf16),
            pltpu.VMEM((16, D), f32),
            pltpu.VMEM((D, 3 * D), f32),
            pltpu.VMEM((D, D), f32),
            pltpu.VMEM((D, FF), f32),
            pltpu.VMEM((FF, D), f32),
            pltpu.VMEM((2,) + bout.shape, bf16),
            sems((13,)),
            sems((12,)),
            sems((2, 2)),
        ],
        compiler_params=pltpu.CompilerParams(vmem_limit_bytes=64 * 1024 * 1024 - 65536),
    )(bout, gtok, out_g, out_v, stats)
    bout, gtok, g_qkv, g_proj, g_up, g_down, qb, vb, pb, ub, db, g1, s1, g2, s2, stats = outs
    return (bout, stats, gtok, g_qkv, qb, vb, g_proj, pb, g_up, ub, g_down, db, g1, s1, g2, s2)


def finish(
    bout_in,
    gtok_in,
    g_in,
    v_in,
    stats_in,
    bout,
    gtok,
    g_qkv,
    g_proj,
    g_up,
    g_down,
    qb,
    vb,
    pb,
    ub,
    db,
    g1,
    s1,
    g2,
    s2,
    stats,
    g,
    v,
    t_qkv,
    t_proj,
    t_up,
    t_down,
    t_rows,
    in_sem,
    out_sem,
    row_sem,
):
    rows_in = [
        pltpu.make_async_copy(src, t_rows.at[k], row_sem.at[0, k])
        for k, src in enumerate((bout_in, gtok_in))
    ]
    rows_out = [
        pltpu.make_async_copy(t_rows.at[k], dst, row_sem.at[1, k])
        for k, dst in enumerate((bout, gtok))
    ]
    loads = [
        pltpu.make_async_copy(g_in.at[pl.ds(k * D, D)], g.at[pl.ds(k * D, D)], in_sem.at[k])
        for k in range(12)
    ]
    loads.append(pltpu.make_async_copy(v_in, v, in_sem.at[12]))
    for cp in loads:
        cp.start()
    for cp in rows_in:
        cp.start()
    for c in range(stats.shape[0]):
        for k in range(GROUPS):
            stats[c, k] = stats_in[c, 2 * k : 2 * k + 2, :]
    stores = []
    for k in range(12):
        if k in (4, 8):
            rows_in[k // 8].wait()
            rows_out[k // 8].start()
        loads[k].wait()
        part = g[pl.ds(k * D, D), :].astype(f32)
        if k < 9:
            cols = pl.ds((k - 4) * D, D)
            src, dst = (
                (t_down.at[pl.ds(k * D, D)], g_down.at[pl.ds(k * D, D)])
                if k < 4
                else ((t_up.at[:, cols], g_up.at[:, cols]) if k < 8 else (t_proj, g_proj))
            )
            src[...] = part
            stores.append(pltpu.make_async_copy(src, dst, out_sem.at[k]))
            stores[-1].start()
        else:
            for j in range(3):
                at = j * D + (k - 9) * 128
                t_qkv[:, at : at + 128] = part[:, j * 128 : (j + 1) * 128]
    stores.append(pltpu.make_async_copy(t_qkv, g_qkv, out_sem.at[9]))
    stores[-1].start()
    loads[12].wait()
    for k in range(4):
        ub[k * D : (k + 1) * D] = v[V_UB + k]
    table = ((pb, V_PB), (db, V_DB), (g2, V_G2), (s2, V_S2))
    table += ((qb, V_QB), (vb, V_VB), (g1, V_G1), (s1, V_S1))
    for ref, k in table:
        ref[...] = v[k]
    for cp in stores + rows_out:
        cp.wait()


def solution(mesh):
    row = P("clip", "frame", None)
    in_specs = (row, row, P("clip", None, "frame"), P("clip", None)) + (P(),) * 13
    out_specs = (row, P("clip", None, None, None), row) + (P(),) * 13
    step = functools.partial(local, mesh.shape["frame"], mesh.shape["clip"] // 2)
    return jax.shard_map(step, mesh=mesh, in_specs=in_specs, out_specs=out_specs, check_vma=False)
```

time: 210 us -> 141 us (0.67)
  Pallas kernels: 182 us -> 140 us
  local copies, waits for them, and re-layouts: 19.7 us -> 0 us
  other arithmetic: 7.44 us -> 0 us
    pallas_call x1 -> x2, Pallas kernels: 182 us -> 140 us  [the longest x1 132 us: local(): pl.pallas_call(functools.partial(body, nf, nz), out_shape=(jax.ShapeDtype...]
    unnamed x18 -> x0, local copies, waits for them, and re-layouts: 11.5 us -> none
    convert_element_type x4 -> x0, other arithmetic: 7.29 us -> none  [the longest x1 3.28 us: local(): out_a[0:FF].astype(f32)]
    convert_element_type x3 -> x0, local copies, waits for them, and re-layouts: 4.09 us -> none  [the longest x2 3.48 us: side(): block.reshape(n, D, D).transpose(1, 0, 2).reshape(D, n * D).astype(f32)]
    slice x1 -> x0, local copies, waits for them, and re-layouts: 2.17 us -> none  [local(): out_b[0:3 * D]]
where the time goes in v2:
time: 141 us
  Pallas kernels  140 us (99%)
    pallas_call x1, Pallas kernels, local(): pl.pallas_call(functools.partial(body, nf, nz), out_shape=(jax.ShapeDtype...  132 us
    pallas_call x1, Pallas kernels, local(): pl.pallas_call(finish, out_shape=(shape(bout.shape, bf16), shape(gtok.sha...  7.81 us

profile of v2, /device:TPU:0, one launch (start us, length us, event | category | flops | bytes accessed | tf_op | source)
XLA Modules:
  0.0 140.7 jit_solution(11920058449815701820)
XLA Ops:
  0.7 132.0 %shard_map.288 = (bf16[4,392,384]{2,1,0:T(8,128)(2,1)}, f32[4,4,384]{2,1,0:T(4,128)}, bf16[4,392,384]{2,1,0:T(8,128)(2,1)}, bf16[4608,384]{1,0:T(8,128)(2,1)}, f32[16,384]{1,0:T(8,128)}) custom-call(bf16[4,392,384]{2,1,0:T(8,128)(2,1)} %tok.1, bf16[4,392,384]{2,1,0:T(8,128)(2,1)} %og.1, s32[4,2,392]{2,1,0:T(2,128)} %masks.1, s32[2,4]{1,0:T(2,128)} %bitcast.1, ...), custom_call_target="tpu_custom_call" | custom-call | tf_op jit(solution)/shard_map/pallas_call | solution.py:991
  132.7 7.8 %shard_map.289 = (bf16[4,392,384]{2,1,0:T(8,128)(2,1)}, bf16[4,392,384]{2,1,0:T(8,128)(2,1)}, f32[384,1152]{1,0:T(8,128)}, f32[384,384]{1,0:T(8,128)}, f32[384,1...) custom-call(bf16[4,392,384]{2,1,0:T(8,128)(2,1)} %get-tuple-element., ...), custom_call_target="tpu_custom_call" | custom-call | tf_op jit(solution)/shard_map/pallas_call | solution.py:1082

commit v3 on v2

--- a/solution.py
+++ b/solution.py
@@ -239,10 +239,10 @@
     og,
     masks,
     grp,
-    wqkv,
-    wp,
-    wu,
-    wd,
+    wqkv_in,
+    wp_in,
+    wu_in,
+    wd_in,
     vqb,
     vvb,
     vpb,
@@ -257,6 +257,10 @@
     gtok,
     out_g,
     out_v,
+    wqkv,
+    wp,
+    wu,
+    wd,
     wqvT,
     wpT,
     wuT,
@@ -315,6 +319,7 @@
     out_sem,
     in_sem,
     row_sem,
+    weight_sem,
 ):
     clips = tok.shape[0]
     rows = tok.shape[1]
@@ -335,6 +340,12 @@
 
     for c in range(clips):
         fetch(tok, 0, c).start()
+    pairs = ((wqkv_in, wqkv), (wp_in, wp), (wu_in, wu), (wd_in, wd))
+    weights = [
+        pltpu.make_async_copy(src, dst, weight_sem.at[k]) for k, (src, dst) in enumerate(pairs)
+    ]
+    for cp in weights:
+        cp.start()
 
     NR[...] = jnp.zeros(NR.shape, bf16)
     for c in range(clips):
@@ -450,6 +461,8 @@
     each_side(True, lambda right: (nr_copy(0, right),))
     for c in range(1, clips):
         fetch(tok, 0, c).wait()
+    for cp in weights:
+        cp.wait()
     for n in range(1, max(clips, 5)):
         if n < clips:
             norm_one(n)
@@ -737,9 +750,6 @@
     def gather_rows(row, k):
         VS[row : row + 1, :] = jnp.sum(jnp.transpose(acc[k]), axis=0, keepdims=True)
 
-    gather_rows(V_G2, 0)
-    gather_rows(V_S2, 1)
-
     me = (me_f, me_c)
     refs, red_sems = (G, SB, AG, RL), (red_send, red_recv)
     red = [Reduce(k, refs, red_sems, me, nf, nz) for k in range(len(CHUNKS))]
@@ -761,6 +771,8 @@
 
     for cp in sp_copies():
         cp.start()
+    gather_rows(V_G2, 0)
+    gather_rows(V_S2, 1)
 
     has_before = jnp.where(first, 0.0, 1.0).astype(f32)
     has_after = jnp.where(last, 0.0, 1.0).astype(f32)
@@ -997,9 +1009,13 @@
             jax.ShapeDtypeStruct((G_ROWS, D), bf16),
             jax.ShapeDtypeStruct((16, D), f32),
         ),
-        in_specs=[hbm, hbm, vmem, pl.BlockSpec(memory_space=pltpu.SMEM)] + [vmem] * 13,
+        in_specs=[hbm, hbm, vmem, pl.BlockSpec(memory_space=pltpu.SMEM)] + [hbm] * 4 + [vmem] * 9,
         out_specs=(hbm, vmem, hbm, hbm, hbm),
         scratch_shapes=[
+            pltpu.VMEM((D, 3 * D), bf16),
+            pltpu.VMEM((D, D), bf16),
+            pltpu.VMEM((D, FF), bf16),
+            pltpu.VMEM((FF, D), bf16),
             pltpu.VMEM((2 * D, D), bf16),
             pltpu.VMEM((D, D), bf16),
             pltpu.VMEM((FF, D), bf16),
@@ -1058,6 +1074,7 @@
             sems((len(CHUNKS) + 1,)),
             sems((2, clips)),
             sems((2,)),
+            sems((4,)),
         ],
         compiler_params=pltpu.CompilerParams(
             collective_id=0, has_side_effects=True, vmem_limit_bytes=64 * 1024 * 1024 - 65536

time: 141 us -> 140 us (level)
  no operation moved by 1% of the time
where the time goes in v3:
time: 140 us
  Pallas kernels  139 us (99%)
    pallas_call x1, Pallas kernels, local(): pl.pallas_call(functools.partial(body, nf, nz), out_shape=(jax.ShapeDtype...  131 us
    pallas_call x1, Pallas kernels, local(): pl.pallas_call(finish, out_shape=(shape(bout.shape, bf16), shape(gtok.sha...  7.81 us

profile of v3, /device:TPU:0, one launch (start us, length us, event | category | flops | bytes accessed | tf_op | source)
XLA Modules:
  0.0 139.5 jit_solution(11854902506550978767)
XLA Ops:
  0.7 130.9 %shard_map.288 = (bf16[4,392,384]{2,1,0:T(8,128)(2,1)}, f32[4,4,384]{2,1,0:T(4,128)}, bf16[4,392,384]{2,1,0:T(8,128)(2,1)}, bf16[4608,384]{1,0:T(8,128)(2,1)}, f32[16,384]{1,0:T(8,128)}) custom-call(bf16[4,392,384]{2,1,0:T(8,128)(2,1)} %tok.1, bf16[4,392,384]{2,1,0:T(8,128)(2,1)} %og.1, s32[4,2,392]{2,1,0:T(2,128)} %masks.1, s32[2,4]{1,0:T(2,128)} %bitcast.1, ...), custom_call_target="tpu_custom_call" | custom-call | tf_op jit(solution)/shard_map/pallas_call | solution.py:1003
  131.5 7.8 %shard_map.289 = (bf16[4,392,384]{2,1,0:T(8,128)(2,1)}, bf16[4,392,384]{2,1,0:T(8,128)(2,1)}, f32[384,1152]{1,0:T(8,128)}, f32[384,384]{1,0:T(8,128)}, f32[384,1...) custom-call(bf16[4,392,384]{2,1,0:T(8,128)(2,1)} %get-tuple-element., ...), custom_call_target="tpu_custom_call" | custom-call | tf_op jit(solution)/shard_map/pallas_call | solution.py:1099
